TPU v7x, 256 devices: a whole 4x4x8 slice. The times are simulated.
256 devices in a mesh: dom: 64 (over z, y, core), rep: 4 (over x).
Axes of the slice: x: 4, y: 4, z: 8, core: 2. Of those that a mesh axis runs over, the one named last changes fastest.
Arguments:
- node_input: bfloat16 [1048576, 256], P(('dom', 'rep')), may hold values from -6 to 6
- neighbor_first: int32 [262144, 15], P(('dom', 'rep')), may hold values from 0 to 4095
- neighbor_second: int32 [32768, 10], P(('dom', 'rep')), may hold values from 0 to 1023
- merge_ids: int32 [256, 4096], P(('dom', 'rep')), may hold values from 0 to 2047, never falling along the last dimension, each value on 1 to 4 neighbouring positions
- owner_ids: int32 [524288, 1], P(('dom', 'rep')), may hold values from 0 to 63; in each aligned block of 2048 rows (0 to 2047, 2048 to 4095, ...) at most 40 rows name the same one
- owner_rows: int32 [524288], P(('dom', 'rep')), may hold values from 0 to 2047
- cotangent: bfloat16 [32768, 256], P(('dom', 'rep')), may hold values from -6 to 6
- self_first: bfloat16 [256, 256], replicated, may hold values from -0.375 to 0.375
- agg_first: bfloat16 [256, 256], replicated, may hold values from -0.375 to 0.375
- self_second: bfloat16 [256, 256], replicated, may hold values from -0.375 to 0.375
- agg_second: bfloat16 [256, 256], replicated, may hold values from -0.375 to 0.375
Outputs:
- emb_grad: float32 [131072, 256], P('dom')
- weight_grads: float32 [4, 256, 256], replicated
Inputs may be any that keep to these rules, and one draw needn't show every extreme that they name: `owner_ids`: among one device's 2048 distinct nodes no partition is named more than 40 times, a bound that some block reaches. `merge_ids`: along one device's row the ids never fall; each of the 2048 ids covers 1 to 4 consecutive rows.
All inputs are finite; a program needn't handle non-finite values.
Results may differ from a plain program's by a relative error of at most 0.0042.
Values sent between devices are 32-bit elements; how exact they have to be, the bound alone decides.
No kernel may reach another device: no remote copies, remote signals or barrier semaphores. Data moves between devices by JAX's collectives and lax.ppermute only.
A program may use at most 128 MiB of HBM per device.

v0:
```python
import jax
import jax.numpy as jnp
from jax import lax
from jax.sharding import PartitionSpec as P

ROWS_OWN = 2048


grad_scale = 16.0


def silu_slope(preact):
    sigmoid = jax.nn.sigmoid(preact)
    return sigmoid * (1.0 + preact * (1.0 - sigmoid))


def count_table(indices, columns):
    positions = lax.broadcasted_iota(jnp.int32, (indices.shape[0], columns), 1)
    table = jnp.zeros((indices.shape[0], columns), jnp.bfloat16)
    for column in range(indices.shape[1]):
        table = table + (indices[:, column : column + 1] == positions).astype(jnp.bfloat16)
    return table


def blocked(row_total, function):
    height = min(512, row_total)
    offsets = jnp.arange(row_total // height, dtype=jnp.int32) * height
    results = lax.map(lambda offset: function(offset, height), offsets)
    return results.reshape((row_total,) + results.shape[2:])


def weight_total(g_self1, g_agg1, g_self2, g_agg2, factor):
    totals = lax.psum((g_self1, g_agg1, g_self2, g_agg2), ("dom", "rep"))
    return jnp.stack(totals) * factor


def on_device(
    node_input,
    neighbor_first,
    neighbor_second,
    merge_ids,
    owner_ids,
    owner_rows,
    cotangent,
    self_first,
    agg_first,
    self_second,
    agg_second,
):
    input_total = node_input.shape[0]
    first_total = neighbor_first.shape[0]
    target_total = cotangent.shape[0]
    width = node_input.shape[1]
    fanout_one = neighbor_first.shape[1]
    fanout_two = neighbor_second.shape[1]
    uniq_total = owner_rows.shape[0]
    domains = lax.axis_size("dom")
    factor = (domains * lax.axis_size("rep") * target_total) ** (-0.5)

    def mean_block(offset, height):
        indices = lax.dynamic_slice_in_dim(neighbor_first, offset, height, 0)
        table = count_table(indices, input_total)
        return jnp.dot(table, node_input, preferred_element_type=jnp.float32) / fanout_one

    mean_one = blocked(first_total, mean_block).astype(jnp.bfloat16)
    self_rows = node_input[:first_total]
    preact = jnp.dot(self_rows, self_first, preferred_element_type=jnp.float32) + jnp.dot(
        mean_one, agg_first, preferred_element_type=jnp.float32
    )
    hidden = jax.nn.silu(preact).astype(jnp.bfloat16)
    second_table = count_table(neighbor_second, first_total)
    mean_two = (
        jnp.dot(second_table, hidden, preferred_element_type=jnp.float32) / fanout_two
    ).astype(jnp.bfloat16)
    g_self2 = jnp.dot(hidden[:target_total].T, cotangent, preferred_element_type=jnp.float32)
    g_agg2 = jnp.dot(mean_two.T, cotangent, preferred_element_type=jnp.float32)
    down_two = (
        jnp.dot(cotangent, agg_second.T, preferred_element_type=jnp.float32) / fanout_two
    ).astype(jnp.bfloat16)
    contract_rows = (((0,), (0,)), ((), ()))
    hidden_grad = lax.dot_general(
        second_table, down_two, contract_rows, preferred_element_type=jnp.float32
    )
    hidden_grad = hidden_grad.at[:target_total].add(
        jnp.dot(cotangent, self_second.T, preferred_element_type=jnp.float32)
    )
    pre_grad = (hidden_grad * silu_slope(preact)).astype(jnp.bfloat16)
    g_self1 = jnp.dot(self_rows.T, pre_grad, preferred_element_type=jnp.float32)
    g_agg1 = jnp.dot(mean_one.T, pre_grad, preferred_element_type=jnp.float32)
    down_one = (
        jnp.dot(pre_grad, agg_first.T, preferred_element_type=jnp.float32) / fanout_one
    ).astype(jnp.bfloat16)
    height = min(512, first_total)

    def spread_block(carry, offset):
        indices = lax.dynamic_slice_in_dim(neighbor_first, offset, height, 0)
        table = count_table(indices, input_total)
        grads = lax.dynamic_slice_in_dim(down_one, offset, height, 0)
        return (
            carry
            + lax.dot_general(table, grads, contract_rows, preferred_element_type=jnp.float32),
            None,
        )

    offsets = jnp.arange(first_total // height, dtype=jnp.int32) * height
    spread, _ = lax.scan(spread_block, jnp.zeros((input_total, width), jnp.float32), offsets)
    spread = spread.at[:first_total].add(
        jnp.dot(pre_grad, self_first.T, preferred_element_type=jnp.float32)
    )
    input_grad = spread.astype(jnp.bfloat16)
    row_ids = merge_ids[0]

    def merge_block(offset, span_rows):
        wanted = offset + lax.broadcasted_iota(jnp.int32, (span_rows, input_total), 0)
        picker = (wanted == row_ids[None, :]).astype(jnp.bfloat16)
        return jnp.dot(picker, input_grad, preferred_element_type=jnp.float32)

    merged = blocked(uniq_total, merge_block) * grad_scale
    owners = owner_ids[:, 0]
    capacity = max(2, 5 * uniq_total // (4 * domains))
    marks = (owners[:, None] == lax.broadcasted_iota(jnp.int32, (uniq_total, domains), 1)).astype(
        jnp.int32
    )
    earlier = jnp.cumsum(marks, axis=0) - marks
    slots = jnp.sum(earlier * marks, axis=1)
    targets = owners * capacity + slots
    outgoing = (
        jnp.zeros((domains * capacity, width), jnp.float32)
        .at[targets]
        .set(merged)
        .reshape(domains, capacity, width)
    )
    labels = (
        jnp.full((domains * capacity,), ROWS_OWN, jnp.int32)
        .at[targets]
        .set(owner_rows)
        .reshape(domains, capacity)
    )
    arrived, arrived_rows = (
        lax.all_to_all(outgoing, "dom", split_axis=0, concat_axis=0, tiled=True),
        lax.all_to_all(labels, "dom", split_axis=0, concat_axis=0, tiled=True),
    )
    table = (
        jnp.zeros((ROWS_OWN, width), jnp.float32)
        .at[arrived_rows.reshape(-1)]
        .add(arrived.reshape(-1, width), mode="drop")
    )
    table = lax.psum(table, "rep")
    weight_grads = weight_total(g_self1, g_agg1, g_self2, g_agg2, factor)
    return (table, weight_grads)


def solution(mesh):
    placed = (
        P(("dom", "rep"), None),
        P(("dom", "rep"), None),
        P(("dom", "rep"), None),
        P(("dom", "rep"), None),
        P(("dom", "rep"), None),
        P(("dom", "rep")),
        P(("dom", "rep"), None),
        P(),
        P(),
        P(),
        P(),
    )
    return jax.shard_map(
        on_device, mesh=mesh, in_specs=placed, out_specs=(P("dom", None), P()), check_vma=False
    )
```

profile of v0, /device:TPU:1, one launch (start us, length us, event | category | flops | bytes accessed | tf_op | source)
XLA Modules:
  0.0 546.9 jit_solution(7200130078022077573)
XLA Ops:
  8.0 18.1 %reduce-window.6 = s32[64,16,128]{2,1,0:T(8,128)S(1)} reduce-window(s32[64,16,128]{2,1,0:T(8,128)S(1)} %fusion.153, s32[]{:T(128)} %constant.108.clone.1), window={size=1x1x128 pad=0_0x0_0x127_0}, to_apply=%region_0.1 | reduce-window | flops 16646144 | bytes 1048580 | tf_op jit(solution)/shard_map/reduce-window
  27.5 8.2 %scatter_custom_fusion = s32[2560]{0:T(1024)S(1)} fusion(s32[2048]{0:T(1024)S(1)} %bitcast.236, s32[2048]{0:T(1024)} %param.26, s32[]{:T(128)} %constant.106.clone.1), kind=kCustom, calls=%fused_computation.208 | custom fusion | bytes 10752 | tf_op jit(solution)/shard_map/scatter | solution.py:136
  36.4 13.3 %all-to-all-start = ((s32[64,1,40]{2,1,0:T(1,128)}), s32[64,1,40]{2,1,0:T(1,128)}, u32[]{:S(2)}, u32[]{:S(2)}) async-start(s32[64,1,40]{2,1,0:T(1,128)} %bitcast.27), calls=%async_computation | async-start | bytes 65536 | tf_op jit(solution)/shard_map/all_to_all | solution.py:141
  50.6 41.2 %while.33 = (s32[]{:T(128)}, bf16[2,512,256]{2,1,0:T(8,128)(2,1)S(1)}, s32[2]{0:T(128)S(1)}, s32[1024,15]{0,1:T(8,128)S(1)}, bf16[4096,256]{1,0:T(8,128)(2,1)}, ...) while((s32[]{:T(128)}, ...), condition=%wide.region_5.6_spmd, body=%wide.region_4.5_spmd.sunk | while | flops 1199702016 | bytes 2714075 | solution.py:28
  53.6 17.6 %fusion.216 = bf16[2,512,256]{2,1,0:T(8,128)(2,1)S(1)} fusion(bf16[2,512,256]{2,1,0:T(8,128)(2,1)S(1)} %get-tuple-element.386, s32[]{:T(128)} %get-tuple-element.385, bf16[4096,256]{1,0:T(8,128)(2,1)} %get-tuple-element.411, s32[512]{0:T(512)S(1)} %bitcast.234, s32[512]{0:T(512)S(1)} %bitcast.221, s32[512]{0:T(512)S(1)} %bitcast.222, ...), kind=kOutput, calls=%fused_computation.65.clone.1 | convolution fusion | flops 1199702016 | bytes 2652164 | tf_op jit(solution)/shard_map/while/body/eval_jaxpr/dot_general | solution.py:63
  74.2 17.6 %fusion.216 = bf16[2,512,256]{2,1,0:T(8,128)(2,1)S(1)} fusion(bf16[2,512,256]{2,1,0:T(8,128)(2,1)S(1)} %get-tuple-element.386, s32[]{:T(128)} %get-tuple-element.385, bf16[4096,256]{1,0:T(8,128)(2,1)} %get-tuple-element.411, s32[512]{0:T(512)S(1)} %bitcast.234, s32[512]{0:T(512)S(1)} %bitcast.221, s32[512]{0:T(512)S(1)} %bitcast.222, ...), kind=kOutput, calls=%fused_computation.65.clone.1 | convolution fusion | flops 1199702016 | bytes 2652164 | tf_op jit(solution)/shard_map/while/body/eval_jaxpr/dot_general | solution.py:63
  91.9 1.6 fusion.165
  94.8 1.4 multiply_convert_fusion
  96.6 57.5 %while.35 = (s32[]{:T(128)}, f32[4096,256]{1,0:T(8,128)}, s32[2]{0:T(128)S(1)}, s32[1024,15]{0,1:T(8,128)S(1)}, bf16[1024,256]{1,0:T(8,128)(2,1)S(1)}, /*index=5...) while((s32[]{:T(128)}, f32[4096,256]{1,0:T(8,128)}, ...), condition=%wide.region_7.8_spmd.clone, body=%wide.region_6.7_spmd.clone.sunk | while | flops 1201668096 | bytes 8743397 | solution.py:106
  111.7 18.6 %convolution_add_fusion.5 = f32[4096,256]{1,0:T(8,128)} fusion(f32[4096,256]{1,0:T(8,128)} %get-tuple-element.452, s32[512]{0:T(512)S(1)} %bitcast.219, s32[512]{0:T(512)S(1)} %bitcast.206, s32[512]{0:T(512)S(1)} %bitcast.207, s32[512]{0:T(512)S(1)} %bitcast.208, s32[512]{0:T(512)S(1)} %bitcast.209, s32[512]{0:T(512)S(1)} %bitcast.210, ...), kind=kOutput, calls=%fused_computation.104.clone.1 | convolution fusion | flops 1201668096 | bytes 8681477 | tf_op jit(solution)/shard_map/while/body/eval_jaxpr/dot_general | solution.py:101
  133.1 20.8 %convolution_add_fusion.5 = f32[4096,256]{1,0:T(8,128)} fusion(f32[4096,256]{1,0:T(8,128)} %get-tuple-element.452, s32[512]{0:T(512)S(1)} %bitcast.219, s32[512]{0:T(512)S(1)} %bitcast.206, s32[512]{0:T(512)S(1)} %bitcast.207, s32[512]{0:T(512)S(1)} %bitcast.208, s32[512]{0:T(512)S(1)} %bitcast.209, s32[512]{0:T(512)S(1)} %bitcast.210, ...), kind=kOutput, calls=%fused_computation.104.clone.1 | convolution fusion | flops 1201668096 | bytes 8681477 | tf_op jit(solution)/shard_map/while/body/eval_jaxpr/dot_general | solution.py:101
  154.1 2.5 fusion.140
  156.7 2.4 convert_element_type.169
  159.1 13.3 %while.34 = (s32[]{:T(128)}, f32[4,512,256]{2,1,0:T(8,128)}, s32[4]{0:T(128)S(1)}, s32[1,4096]{1,0:T(1,128)S(1)}, bf16[4096,256]{1,0:T(8,128)(2,1)S(1)}, /*index=5*/s32[]{:T(128)}) while((s32[]{:T(128)}, f32[4,512,256]{2,1,0:T(8,128)}, s32[4]{0:T(128)S(1)}, s32[1,4096]{1,0:T(1,128)S(1)}, bf16[4096,256]{1,0:T(8,128)(2,1)S(1)}, ...), condition=%wide.region_9.10_spmd, body=%wide.region_8.9_spmd.sunk | while | flops 1075839488 | bytes 2642517 | solution.py:28
  160.3 2.1 fusion.219
  163.6 2.1 fusion.219
  167.0 2.1 fusion.219
  170.3 2.1 fusion.219
  172.4 1.8 broadcast_multiply_fusion
  174.2 10.8 %scatter_custom_fusion.1 = f32[2560,256]{1,0:T(8,128)} fusion(s32[2048]{0:T(1024)} %bitcast.237, f32[2048,256]{1,0:T(8,128)S(1)} %bitcast.197, f32[]{:T(128)} %constant.105.clone.1), kind=kCustom, calls=%fused_computation.141 | custom fusion | bytes 2621952 | tf_op jit(solution)/shard_map/scatter | solution.py:130
  185.1 10.3 %all-to-all-start.1 = ((f32[64,40,256]{2,1,0:T(8,128)}), f32[64,40,256]{2,1,0:T(8,128)S(1)}, u32[]{:S(2)}, u32[]{:S(2)}) async-start(f32[64,40,256]{2,1,0:T(8,128)} %bitcast.40), calls=%async_computation.1 | async-start | bytes 5242880 | tf_op jit(solution)/shard_map/all_to_all | solution.py:140
  195.4 1.8 convolution_bitcast_fusion.3
  197.2 2.1 convolution_bitcast_fusion
  199.3 2.1 convolution_bitcast_fusion.1
  201.5 2.8 convolution_bitcast_fusion.2
  204.9 1.5 reduce.9
  206.5 52.4 %all-to-all-done.1 = f32[64,40,256]{2,1,0:T(8,128)S(1)} async-done(((f32[64,40,256]{2,1,0:T(8,128)}), f32[64,40,256]{2,1,0:T(8,128)S(1)}, u32[]{:S(2)}, u32[]{:S(2)}) %all-to-all-start.1) | async-done | bytes 2621472 | tf_op jit(solution)/shard_map/all_to_all | solution.py:140
  258.9 15.7 %scatter_custom_fusion.2 = f32[2048,256]{1,0:T(8,128)} fusion(s32[2560]{0:T(1024)S(1)} %fusion.182, f32[2560,256]{1,0:T(8,128)S(1)} %bitcast.196, f32[]{:T(128)} %constant.105.clone.1), kind=kCustom, calls=%fused_computation.160 | custom fusion | flops 655360 | bytes 2097156 | tf_op jit(solution)/shard_map/scatter-add | solution.py:146
  274.6 195.3 %all-reduce.6.cloned.1.call-done = (f32[1,256,256]{1,2,0:T(8,128)}, f32[1,256,256]{1,2,0:T(8,128)}, f32[1,256,256]{1,2,0:T(8,128)}, f32[1,256,256]{1,2,0:T(8,128)}) async-done(((f32[1,256,256]{1,2,0:T(8,128)}, f32[1,256,256]{1,2,0:T(8,128)}, f32[1,256,256]{1,2,0:T(8,128)}, f32[1,256,256]{1,2,0:T(8,128)}), (f32[1,256,256]{1,2,0:T(8,128)}, f32[1,256,256]{1,2,0:T(8,128)}, f32[1,256,256]{1,2,0:T(8,128)}, ...) | async-done | bytes 1048592 | tf_op jit(solution)/shard_map/psum | solution.py:33
  471.2 1.3 copy.29
  472.5 64.2 %all-reduce.4.cloned.1.call-done = f32[2048,256]{1,0:T(8,128)} async-done(((f32[2048,256]{1,0:T(8,128)}), f32[2048,256]{1,0:T(8,128)}) %all-reduce.4.cloned.1.call-update) | async-done | bytes 2097168 | tf_op jit(solution)/shard_map/psum | solution.py:148
  536.8 3.0 copy.63
  (108 shorter events, 15.4 us)
Async XLA Ops:
  7.2 84.7 %copy-start = (bf16[256,256]{1,0:T(8,128)(2,1)S(1)}, bf16[256,256]{1,0:T(8,128)(2,1)}, u32[]{:S(2)}) copy-start(bf16[256,256]{1,0:T(8,128)(2,1)} %param.28) | copy-start | bytes 393220
  7.2 20.0 %copy-start.7 = (s32[2048,1]{0,1:T(1,128)S(1)}, s32[2048,1]{0,1:T(1,128)}, u32[]{:S(2)}) copy-start(s32[2048,1]{0,1:T(1,128)} %param.25) | copy-start | bytes 24580
  7.2 43.2 %copy-start.9 = (s32[128,10]{0,1:T(8,128)S(1)}, s32[128,10]{0,1:T(8,128)}, u32[]{:S(2)}) copy-start(s32[128,10]{0,1:T(8,128)} %param.23) | copy-start | bytes 15364
  7.2 43.2 %copy-start.1 = (s32[1024,15]{0,1:T(8,128)S(1)}, s32[1024,15]{0,1:T(8,128)}, u32[]{:S(2)}) copy-start(s32[1024,15]{0,1:T(8,128)} %param.22) | copy-start | bytes 184324
  27.5 22.9 %copy-start.8 = (s32[2048,1]{0,1:T(1,128)}, s32[2048,1]{0,1:T(1,128)S(1)}, u32[]{:S(2)}) copy-start(s32[2048,1]{0,1:T(1,128)S(1)} %compare_select_fusion.1) | copy-start | bytes 24580
  36.4 148.6 %all-to-all-start = ((s32[64,1,40]{2,1,0:T(1,128)}), s32[64,1,40]{2,1,0:T(1,128)}, u32[]{:S(2)}, u32[]{:S(2)}) async-start(s32[64,1,40]{2,1,0:T(1,128)} %bitcast.27), calls=%async_computation | async-start | bytes 65536 | tf_op jit(solution)/shard_map/all_to_all | solution.py:141
  50.4 43.0 %copy-start.10 = (s32[128]{0:T(128)}, s32[128]{0:T(128)S(1)}, u32[]{:S(2)}) copy-start(s32[128]{0:T(128)S(1)} %get-tuple-element.200) | copy-start | bytes 1540
  50.5 43.0 %copy-start.12 = (s32[128]{0:T(128)}, s32[128]{0:T(128)S(1)}, u32[]{:S(2)}) copy-start(s32[128]{0:T(128)S(1)} %get-tuple-element.201) | copy-start | bytes 1540
  50.5 43.0 %copy-start.14 = (s32[128]{0:T(128)}, s32[128]{0:T(128)S(1)}, u32[]{:S(2)}) copy-start(s32[128]{0:T(128)S(1)} %get-tuple-element.202) | copy-start | bytes 1540
  50.5 43.0 %copy-start.16 = (s32[128]{0:T(128)}, s32[128]{0:T(128)S(1)}, u32[]{:S(2)}) copy-start(s32[128]{0:T(128)S(1)} %get-tuple-element.203) | copy-start | bytes 1540
  50.5 43.0 %copy-start.18 = (s32[128]{0:T(128)}, s32[128]{0:T(128)S(1)}, u32[]{:S(2)}) copy-start(s32[128]{0:T(128)S(1)} %get-tuple-element.204) | copy-start | bytes 1540
  50.5 43.0 %copy-start.20 = (s32[128]{0:T(128)}, s32[128]{0:T(128)S(1)}, u32[]{:S(2)}) copy-start(s32[128]{0:T(128)S(1)} %get-tuple-element.205) | copy-start | bytes 1540
  50.5 43.0 %copy-start.22 = (s32[128]{0:T(128)}, s32[128]{0:T(128)S(1)}, u32[]{:S(2)}) copy-start(s32[128]{0:T(128)S(1)} %get-tuple-element.206) | copy-start | bytes 1540
  50.5 43.0 %copy-start.24 = (s32[128]{0:T(128)}, s32[128]{0:T(128)S(1)}, u32[]{:S(2)}) copy-start(s32[128]{0:T(128)S(1)} %get-tuple-element.207) | copy-start | bytes 1540
  50.5 43.0 %copy-start.26 = (s32[128]{0:T(128)}, s32[128]{0:T(128)S(1)}, u32[]{:S(2)}) copy-start(s32[128]{0:T(128)S(1)} %get-tuple-element.208) | copy-start | bytes 1540
  50.5 43.0 %copy-start.28 = (s32[128]{0:T(128)}, s32[128]{0:T(128)S(1)}, u32[]{:S(2)}) copy-start(s32[128]{0:T(128)S(1)} %get-tuple-element.209) | copy-start | bytes 1540
  50.5 43.0 %copy-start.3 = (bf16[128,256]{1,0:T(8,128)(2,1)S(1)}, bf16[128,256]{1,0:T(8,128)(2,1)}, u32[]{:S(2)}) copy-start(bf16[128,256]{1,0:T(8,128)(2,1)} %param.27) | copy-start | bytes 196612
  50.6 43.0 %copy-start.30 = (bf16[256,256]{1,0:T(8,128)(2,1)S(1)}, bf16[256,256]{1,0:T(8,128)(2,1)}, u32[]{:S(2)}) copy-start(bf16[256,256]{1,0:T(8,128)(2,1)} %param.31) | copy-start | bytes 393220
  174.2 21.3 %copy-start.4 = (bf16[128,256]{1,0:T(8,128)(2,1)S(1)}, bf16[128,256]{1,0:T(8,128)(2,1)}, u32[]{:S(2)}) copy-start(bf16[128,256]{1,0:T(8,128)(2,1)} %param.27) | copy-start | bytes 196612
  185.0 16.4 %copy-start.11 = (s32[128]{0:T(128)S(1)}, s32[128]{0:T(128)}, u32[]{:S(2)}) copy-start(s32[128]{0:T(128)} %copy-done.10) | copy-start | bytes 1540
  185.0 16.4 %copy-start.13 = (s32[128]{0:T(128)S(1)}, s32[128]{0:T(128)}, u32[]{:S(2)}) copy-start(s32[128]{0:T(128)} %copy-done.12) | copy-start | bytes 1540
  185.0 16.4 %copy-start.15 = (s32[128]{0:T(128)S(1)}, s32[128]{0:T(128)}, u32[]{:S(2)}) copy-start(s32[128]{0:T(128)} %copy-done.14) | copy-start | bytes 1540
  185.0 16.4 %copy-start.17 = (s32[128]{0:T(128)S(1)}, s32[128]{0:T(128)}, u32[]{:S(2)}) copy-start(s32[128]{0:T(128)} %copy-done.16) | copy-start | bytes 1540
  185.0 16.4 %copy-start.19 = (s32[128]{0:T(128)S(1)}, s32[128]{0:T(128)}, u32[]{:S(2)}) copy-start(s32[128]{0:T(128)} %copy-done.18) | copy-start | bytes 1540
  185.0 16.4 %copy-start.21 = (s32[128]{0:T(128)S(1)}, s32[128]{0:T(128)}, u32[]{:S(2)}) copy-start(s32[128]{0:T(128)} %copy-done.20) | copy-start | bytes 1540
  185.0 16.4 %copy-start.23 = (s32[128]{0:T(128)S(1)}, s32[128]{0:T(128)}, u32[]{:S(2)}) copy-start(s32[128]{0:T(128)} %copy-done.22) | copy-start | bytes 1540
  185.0 16.4 %copy-start.25 = (s32[128]{0:T(128)S(1)}, s32[128]{0:T(128)}, u32[]{:S(2)}) copy-start(s32[128]{0:T(128)} %copy-done.24) | copy-start | bytes 1540
  185.0 16.4 %copy-start.27 = (s32[128]{0:T(128)S(1)}, s32[128]{0:T(128)}, u32[]{:S(2)}) copy-start(s32[128]{0:T(128)} %copy-done.26) | copy-start | bytes 1540
  185.1 16.4 %copy-start.29 = (s32[128]{0:T(128)S(1)}, s32[128]{0:T(128)}, u32[]{:S(2)}) copy-start(s32[128]{0:T(128)} %copy-done.28) | copy-start | bytes 1540
  185.1 73.8 %all-to-all-start.1 = ((f32[64,40,256]{2,1,0:T(8,128)}), f32[64,40,256]{2,1,0:T(8,128)S(1)}, u32[]{:S(2)}, u32[]{:S(2)}) async-start(f32[64,40,256]{2,1,0:T(8,128)} %bitcast.40), calls=%async_computation.1 | async-start | bytes 5242880 | tf_op jit(solution)/shard_map/all_to_all | solution.py:140
  195.4 274.5 %all-reduce.6.cloned.1.call-start = ((), (), s32[]{:S(2)}) async-start(), calls=%async_computation.3 | async-start | bytes 2097152 | tf_op jit(solution)/shard_map/psum | solution.py:33
  204.3 332.5 %all-reduce.4.cloned.1.call-start = ((), (), s32[]{:S(2)}) async-start(), calls=%async_computation.2 | async-start | bytes 4194304 | tf_op jit(solution)/shard_map/psum | solution.py:148
  (5 other events, 20.0 us)
Sparse Core Ops, SparseCore 0:
  204.4 265.4 all-reduce.5
  473.0 63.7 all-reduce.3
where the time goes:
time: 551 us; the launch traced here: 547 us
  waiting for transfers between devices  312 us (57%)
  matrix products  98.8 us (18%)
  other arithmetic  45.4 us (8%)
  local copies, waits for them, and re-layouts  31.2 us (6%)
  starting transfers between devices  23.7 us (4%)
  loops' own time  20.8 us (4%)
  between operations  14.9 us (3%)
    psum x1, waiting for transfers between devices, weight_total(): totals = lax.psum((g_self1, g_agg1, g_self2, g_agg2), ('dom', 'rep'))  195 us
    psum x1, waiting for transfers between devices, on_device(): table = lax.psum(table, 'rep')  64.2 us
    all_to_all x1, waiting for transfers between devices, on_device(): lax.all_to_all(outgoing, 'dom', split_axis=0, concat_axis=0, tiled=True)  52.4 us
    dot_general x2, matrix products, spread_block(): lax.dot_general(table, grads, contract_rows, preferred_element_type=jnp.f...  39.3 us
    dot_general x2, matrix products, mean_block(): jnp.dot(table, node_input, preferred_element_type=jnp.float32) / fanout_one  35.3 us
    another operation x3, other arithmetic  18.5 us
    another operation x1, loops' own time, on_device(): lax.scan(spread_block, jnp.zeros((input_total, width), jnp.float32), offs...  16.5 us
    scatter-add x1, other arithmetic, on_device(): table = jnp.zeros((ROWS_OWN, width), jnp.float32).at[arrived_rows.reshape...  15.7 us
  transfers between devices with their start and end apart: 4, of which 3 were waited for; matrix products, arithmetic and copies ran while one was open for 26% of the time, Pallas kernels for 0%

commit v1 on v0

v1 whole, which is shorter than its diff:
```python
import functools

import jax
import jax.numpy as jnp
from jax import lax
from jax.experimental import pallas as pl
from jax.experimental.pallas import tpu as pltpu
from jax.sharding import PartitionSpec as P

ROWS_OWN = 2048
GRAD_SCALE = 16.0
NIBBLES = 8
NIBBLE_BITS = 4
SPAN = 256
LANES = 128
REPS = 4
F32 = jnp.float32
BF16 = jnp.bfloat16
NN = (((1,), (0,)), ((), ()))
NT = (((1,), (1,)), ((), ()))


def matmul(a, b, dims=NN):
    return lax.dot_general(a, b, dims, preferred_element_type=F32)


def sigmoid(v):
    return 1.0 / (1.0 + jnp.exp(-v))


def local_kernel(
    capacity,
    x_ref,
    first_ref,
    second_ref,
    ids_ref,
    ids_smem,
    owners_ref,
    rows_ref,
    cot_ref,
    self1_ref,
    agg1_ref,
    self2_ref,
    agg2_ref,
    out_ref,
    grads_ref,
    xt_ref,
    table_ref,
    mean_ref,
    down_ref,
    selfgrad_ref,
    spread_ref,
    merged_ref,
    picked_ref,
    target_ref,
    high_ref,
    low_ref,
):
    inputs, width = x_ref.shape
    fan1, firsts = first_ref.shape
    fan2, batch = second_ref.shape
    uniq = owners_ref.shape[1]
    domains = high_ref.shape[0]
    words = inputs // NIBBLES
    lanes = 128
    depth = 64

    eye = (
        lax.broadcasted_iota(jnp.int32, (width, width), 0)
        == lax.broadcasted_iota(jnp.int32, (width, width), 1)
    ).astype(BF16)

    def turn(c, _):
        at = pl.multiple_of(c * 512, 512)
        xt_ref[:, pl.ds(at, 512)] = matmul(eye, x_ref[pl.ds(at, 512), :], NT).astype(BF16)
        return 0

    lax.fori_loop(0, inputs // 512, turn, 0)

    def count(step, _):
        col = pl.multiple_of((step // (words // depth)) * lanes, lanes)
        row = pl.multiple_of((step % (words // depth)) * depth, depth)
        nodes = first_ref[:, pl.ds(col, lanes)]
        keys = nodes % words
        values = jnp.left_shift(jnp.int32(1), (nodes // words) * NIBBLE_BITS)
        place = lax.broadcasted_iota(jnp.int32, (depth, lanes), 0) + row
        total = jnp.zeros((depth, lanes), jnp.int32)
        for k in range(fan1):
            total = total + jnp.where(keys[k : k + 1, :] == place, values[k : k + 1, :], 0)
        for part in range(NIBBLES):
            counts = jnp.bitwise_and(jnp.right_shift(total, part * NIBBLE_BITS), 15)
            table_ref[pl.ds(part * words + row, depth), pl.ds(col, lanes)] = counts.astype(
                F32
            ).astype(BF16)
        return 0

    lax.fori_loop(0, (firsts // lanes) * (words // depth), count, 0)

    def mean(c, _):
        at = pl.multiple_of(c * SPAN, SPAN)
        mean_ref[:, pl.ds(at, SPAN)] = (
            matmul(xt_ref[...], table_ref[:, pl.ds(at, SPAN)]) / fan1
        ).astype(BF16)
        return 0

    lax.fori_loop(0, firsts // SPAN, mean, 0)

    mean_one = mean_ref[...]
    selfs = xt_ref[:, :firsts]
    contract_first = (((0,), (0,)), ((), ()))
    preact = matmul(self1_ref[...], selfs, contract_first) + matmul(
        agg1_ref[...], mean_one, contract_first
    )
    gate = sigmoid(preact)
    hidden = (preact * gate).astype(BF16)
    second = jnp.zeros((firsts, batch), F32)
    place2 = lax.broadcasted_iota(jnp.int32, (firsts, batch), 0)
    for k in range(fan2):
        second = second + (second_ref[k : k + 1, :] == place2).astype(F32)
    second = second.astype(BF16)
    mean_two = (matmul(hidden, second) / fan2).astype(BF16)
    cot = cot_ref[...]
    grads_ref[2 * width : 3 * width, :] = matmul(hidden[:, :batch], cot)
    grads_ref[3 * width :, :] = matmul(mean_two, cot)
    down_two = (matmul(agg2_ref[...], cot, NT) / fan2).astype(BF16)
    hidden_grad = matmul(down_two, second, NT)
    targets_grad = hidden_grad[:, :batch] + matmul(self2_ref[...], cot, NT)
    hidden_grad = jnp.concatenate([targets_grad, hidden_grad[:, batch:]], axis=1)
    pre_grad = (hidden_grad * (gate * (1.0 + preact * (1.0 - gate)))).astype(BF16)
    grads_ref[:width, :] = matmul(selfs, pre_grad, NT)
    grads_ref[width : 2 * width, :] = matmul(mean_one, pre_grad, NT)
    down_ref[...] = (matmul(agg1_ref[...], pre_grad) / fan1).astype(BF16)
    selfgrad_ref[...] = matmul(self1_ref[...], pre_grad)

    step_rows = 512
    for c in range(firsts // step_rows):
        at = c * step_rows
        spread_ref[:, at : at + step_rows] = (
            matmul(down_ref[...], table_ref[at : at + step_rows, :], NT)
            + selfgrad_ref[:, at : at + step_rows]
        ).astype(BF16)

    def spread(c, _):
        at = pl.multiple_of(c * step_rows, step_rows)
        spread_ref[:, pl.ds(at, step_rows)] = matmul(
            down_ref[...], table_ref[pl.ds(at, step_rows), :], NT
        ).astype(BF16)
        return 0

    lax.fori_loop(firsts // step_rows, inputs // step_rows, spread, 0)

    window = SPAN + 8
    merged_ref[...] = jnp.zeros(merged_ref.shape, F32)

    def merge(c, _):
        at = pl.multiple_of(c * SPAN, SPAN)
        low = jnp.minimum(ids_smem[0, at] // 8, (uniq - window) // 8) * 8
        low = pl.multiple_of(low, 8)
        place = lax.broadcasted_iota(jnp.int32, (window, SPAN), 0) + low
        picker = (ids_ref[:, pl.ds(at, SPAN)] == place).astype(F32).astype(BF16)
        merged_ref[pl.ds(low, window), :] += matmul(picker, spread_ref[:, pl.ds(at, SPAN)], NT)
        return 0

    lax.fori_loop(0, inputs // SPAN, merge, 0)
    picked_ref[...] = (merged_ref[...] * GRAD_SCALE).astype(BF16)

    upper = (
        lax.broadcasted_iota(jnp.int32, (SPAN, SPAN), 0)
        < lax.broadcasted_iota(jnp.int32, (SPAN, SPAN), 1)
    ).astype(BF16)
    domain = lax.broadcasted_iota(jnp.int32, (domains, SPAN), 0)
    half = capacity // 2
    tall = half + 1
    slot_place = lax.broadcasted_iota(jnp.int32, (LANES, SPAN), 0)
    carry = jnp.zeros((domains, 1), F32)
    high = jnp.zeros((domains, LANES), F32)
    low = jnp.zeros((domains, LANES), F32)
    for c in range(uniq // SPAN):
        at = c * SPAN
        owners = owners_ref[:, at : at + SPAN]
        marks = (owners == domain).astype(F32)
        marks_b = marks.astype(BF16)
        earlier = matmul(marks_b, upper) + carry
        slots = jnp.sum(earlier * marks, axis=0, keepdims=True).astype(jnp.int32)
        carry = carry + jnp.sum(marks, axis=1, keepdims=True)
        base = owners * tall + slots
        target_ref[0:1, at : at + SPAN] = jnp.where(slots < half, base, -1)
        target_ref[1:2, at : at + SPAN] = jnp.where(slots < half, -1, base - half)
        codes = rows_ref[:, at : at + SPAN] + 1
        here = slots == slot_place
        high = high + matmul(marks_b, jnp.where(here, codes // 16, 0).astype(F32).astype(BF16), NT)
        low = low + matmul(marks_b, jnp.where(here, codes % 16, 0).astype(F32).astype(BF16), NT)
    high_ref[...] = high
    low_ref[...] = low

    group = 8
    chunk = group * tall
    quarter = width // REPS
    label_line = (
        lax.broadcasted_iota(jnp.int32, (chunk, group), 0)
        == lax.broadcasted_iota(jnp.int32, (chunk, group), 1) * tall + half
    ).astype(F32).astype(BF16)

    def place_rows(c, _):
        at = pl.multiple_of(c * chunk, chunk)
        doms = pl.ds(pl.multiple_of(c * group, group), group)
        place = lax.broadcasted_iota(jnp.int32, (chunk, uniq), 0) + at
        first_half = matmul(
            (target_ref[0:1, :] == place).astype(F32).astype(BF16), picked_ref[...]
        )
        second_half = matmul(
            (target_ref[1:2, :] == place).astype(F32).astype(BF16), picked_ref[...]
        )
        labels = matmul(label_line, high_ref[doms, :].astype(BF16)) * 16.0 + matmul(
            label_line, low_ref[doms, :].astype(BF16)
        )
        for r in range(REPS):
            columns = slice(r * quarter, (r + 1) * quarter)
            line = jnp.concatenate([first_half[:, columns], second_half[:, columns]], axis=1)
            out_ref[pl.ds(pl.multiple_of(r * domains * tall + at, 8), chunk), :] = line + labels
        return 0

    lax.fori_loop(0, domains // group, place_rows, 0)


def add_kernel(capacity, lines_ref, table_ref):
    half = capacity // 2
    tall = half + 1
    group = 32
    chunk = group * tall
    sources = lines_ref.shape[0] // tall
    quarter = LANES // 2
    height = table_ref.shape[0]

    def spot(shape, axis):
        index = lax.broadcasted_iota(jnp.int32, shape, axis)
        source = index // tall
        return source, index - source * tall

    def one(mask):
        return mask.astype(F32).astype(BF16)

    line_source, line_slot = spot((LANES, chunk), 1)
    lane = lax.broadcasted_iota(jnp.int32, (LANES, chunk), 0)
    real = line_slot < half
    spread_first = one((lane == line_slot) & real)
    spread_second = one((lane == line_slot + half) & real)
    mine = line_source[:group, :] == lax.broadcasted_iota(jnp.int32, (group, chunk), 0)
    col_source, _ = spot((chunk, group), 0)
    expand = one(col_source == lax.broadcasted_iota(jnp.int32, (chunk, group), 1))
    _, col_slot = spot((chunk, LANES), 0)
    col_lane = lax.broadcasted_iota(jnp.int32, (chunk, LANES), 1)
    col_real = col_slot < half
    at_first = (col_lane == col_slot) & col_real
    at_second = (col_lane == col_slot + half) & col_real
    left = col_lane < quarter
    place = lax.broadcasted_iota(jnp.int32, (height, chunk), 0)
    table_ref[...] = jnp.zeros(table_ref.shape, F32)

    def step(c, _):
        at = pl.multiple_of(c * chunk, 8)
        codes = lines_ref[pl.ds(at + half, group, stride=tall), :]
        lines = lines_ref[pl.ds(at, chunk), :]
        swapped = pltpu.roll(lines, quarter, 1)
        high = jnp.floor(codes * (1.0 / 16.0))
        low = (codes - high * 16.0).astype(BF16)
        high = high.astype(BF16)
        grown = matmul(expand, high) * 16.0 + matmul(expand, low)
        total = jnp.zeros(table_ref.shape, F32)
        for spread, at_column, pair in (
            (spread_first, at_first, jnp.where(left, lines, swapped)),
            (spread_second, at_second, jnp.where(left, swapped, lines)),
        ):
            flat = matmul(high, spread) * 16.0 + matmul(low, spread)
            row = jnp.sum(jnp.where(mine, flat, 0.0), axis=0, keepdims=True).astype(jnp.int32) - 1
            column = jnp.sum(jnp.where(at_column, grown, 0.0), axis=1, keepdims=True)
            column = column.astype(jnp.int32) - 1
            block = jnp.where(column < 0, -1, jnp.right_shift(column, 9))
            kept = [
                jnp.where(block == 2 * side + jnp.where(left, 0, 1), pair, 0.0).astype(BF16)
                for side in range(2)
            ]
            wide = jnp.concatenate(kept, axis=1)
            picker = one((row & (height - 1)) == place)
            total = total + matmul(picker, wide)
        table_ref[...] += total
        return 0

    lax.fori_loop(0, sources // group, step, 0)


def join_kernel(parts_ref, table_ref):
    height = parts_ref.shape[0] // REPS
    quarter = parts_ref.shape[1] // REPS
    for q in range(REPS):
        table_ref[q * height : (q + 1) * height, :] = jnp.concatenate(
            [
                parts_ref[r * height : (r + 1) * height, q * quarter : (q + 1) * quarter]
                for r in range(REPS)
            ],
            axis=1,
        )


VMEM = pl.BlockSpec(memory_space=pltpu.VMEM)
SMEM = pl.BlockSpec(memory_space=pltpu.SMEM)
PARAMS = pltpu.CompilerParams(vmem_limit_bytes=48 * 1024 * 1024)


def local_pass(capacity, domains, x, first, second, ids, owners, rows, cot, self1, agg1, self2, agg2):
    inputs, width = x.shape
    firsts = first.shape[1]
    uniq = owners.shape[1]
    return pl.pallas_call(
        functools.partial(local_kernel, capacity),
        out_shape=(
            jax.ShapeDtypeStruct((REPS * domains * (capacity // 2 + 1), LANES), F32),
            jax.ShapeDtypeStruct((4 * width, width), F32),
        ),
        in_specs=[VMEM] * 4 + [SMEM] + [VMEM] * 7,
        out_specs=(VMEM, VMEM),
        scratch_shapes=[
            pltpu.VMEM((width, inputs), BF16),
            pltpu.VMEM((inputs, firsts), BF16),
            pltpu.VMEM((width, firsts), BF16),
            pltpu.VMEM((width, firsts), BF16),
            pltpu.VMEM((width, firsts), F32),
            pltpu.VMEM((width, inputs), BF16),
            pltpu.VMEM((uniq, width), F32),
            pltpu.VMEM((uniq, width), BF16),
            pltpu.VMEM((2, uniq), jnp.int32),
            pltpu.VMEM((domains, LANES), F32),
            pltpu.VMEM((domains, LANES), F32),
        ],
        compiler_params=PARAMS,
        name="local_pass",
    )(x, first, second, ids, ids, owners, rows, cot, self1, agg1, self2, agg2)


def add_rows(capacity, lines):
    return pl.pallas_call(
        functools.partial(add_kernel, capacity),
        out_shape=jax.ShapeDtypeStruct((ROWS_OWN // REPS, 4 * (LANES // 2)), F32),
        in_specs=[VMEM],
        out_specs=VMEM,
        compiler_params=PARAMS,
        name="add_rows",
    )(lines)


def join_columns(parts):
    return pl.pallas_call(
        join_kernel,
        out_shape=jax.ShapeDtypeStruct(parts.shape, F32),
        in_specs=[VMEM],
        out_specs=VMEM,
        compiler_params=PARAMS,
        name="join_columns",
    )(parts)


def on_device(
    node_input,
    neighbor_first,
    neighbor_second,
    merge_ids,
    owner_ids,
    owner_rows,
    cotangent,
    self_first,
    agg_first,
    self_second,
    agg_second,
):
    target_total = cotangent.shape[0]
    width = node_input.shape[1]
    uniq_total = owner_rows.shape[0]
    domains = lax.axis_size("dom")
    factor = (domains * lax.axis_size("rep") * target_total) ** (-0.5)
    capacity = max(2, 5 * uniq_total // (4 * domains))
    outgoing, grads = local_pass(
        capacity,
        domains,
        node_input,
        neighbor_first.T,
        neighbor_second.T,
        merge_ids,
        owner_ids.T,
        owner_rows[None, :],
        cotangent,
        self_first,
        agg_first,
        self_second,
        agg_second,
    )
    arrived = lax.all_to_all(
        outgoing.reshape(REPS * domains, 1, -1), ("rep", "dom"), 0, 0, tiled=True
    )
    own_grads = lax.psum_scatter(grads, "rep", scatter_dimension=0, tiled=True)
    share = width // domains
    shares = lax.all_to_all(own_grads.reshape(domains, share, width), "dom", 0, 0, tiled=True)
    total = jnp.sum(shares, axis=0) * factor
    whole = lax.all_to_all(
        jnp.broadcast_to(total[None], (domains, share, width)), "dom", 0, 0, tiled=True
    ).reshape(width, width)
    weight_grads = lax.all_to_all(
        jnp.broadcast_to(whole[None], (REPS, width, width)), "rep", 0, 0, tiled=True
    )
    quarter = add_rows(capacity, arrived.reshape(-1, LANES))
    table = join_columns(lax.all_gather(quarter, "rep", axis=0, tiled=True))
    return (table, weight_grads)


def solution(mesh):
    placed = (
        P(("dom", "rep"), None),
        P(("dom", "rep"), None),
        P(("dom", "rep"), None),
        P(("dom", "rep"), None),
        P(("dom", "rep"), None),
        P(("dom", "rep")),
        P(("dom", "rep"), None),
        P(),
        P(),
        P(),
        P(),
    )
    return jax.shard_map(
        on_device, mesh=mesh, in_specs=placed, out_specs=(P("dom", None), P()), check_vma=False
    )
```

time: 551 us -> 211 us (0.38)
  waiting for transfers between devices: 312 us -> 67.2 us
  matrix products: 98.8 us -> 0 us
  blocking collectives: 0 us -> 53.8 us
  other arithmetic: 45.4 us -> 0.09 us
  Pallas kernels: 0 us -> 44.8 us
  loops' own time: 20.8 us -> 0 us
  local copies, waits for them, and re-layouts: 31.2 us -> 14.4 us
  starting transfers between devices: 23.7 us -> 15.7 us
    psum x2 -> x0, waiting for transfers between devices: 260 us -> none  [the longest x1 195 us: weight_total(): totals = lax.psum((g_self1, g_agg1, g_self2, g_agg2), ('dom', 'rep'))]
    dot_general x18 -> x0, matrix products: 98.8 us -> none  [the longest x2 39.3 us: spread_block(): lax.dot_general(table, grads, contract_rows, preferred_element_type=jnp.f...]
    all_to_all x0 -> x3, blocking collectives: none -> 53.8 us  [the longest x1 18.8 us: on_device(): lax.all_to_all(own_grads.reshape(domains, share, width), 'dom', 0, 0, til...]
    pallas_call x0 -> x3, Pallas kernels: none -> 44.8 us  [the longest x1 31.9 us: local_pass(): pl.pallas_call(functools.partial(local_kernel, capacity), out_shape=(jax....]
    another operation x3 -> x0, loops' own time: 20.8 us -> none  [the longest x1 16.5 us: on_device(): lax.scan(spread_block, jnp.zeros((input_total, width), jnp.float32), offs...]
    scatter x2 -> x0, local copies, waits for them, and re-layouts: 19 us -> none  [the longest x1 10.8 us: on_device(): outgoing = jnp.zeros((domains * capacity, width), jnp.float32).at[targets...]
    another operation x3 -> x0, other arithmetic: 18.5 us -> none
    scatter-add x1 -> x0, other arithmetic: 15.7 us -> none  [on_device(): table = jnp.zeros((ROWS_OWN, width), jnp.float32).at[arrived_rows.reshape...]
  transfers between devices with their start and end apart: 4 -> 3, of which waited for: 3 -> 1; matrix products, arithmetic and copies ran while one was open for 26% -> 1% of each run, Pallas kernels for 0% -> 5%
where the time goes in v1:
time: 211 us; the launch traced here: 210 us
  waiting for transfers between devices  67.2 us (32%)
  blocking collectives  53.8 us (25%)
  Pallas kernels  44.8 us (21%)
  starting transfers between devices  15.7 us (7%)
  local copies, waits for them, and re-layouts  14.4 us (7%)
  between operations  14.1 us (7%)
    all_to_all x1, waiting for transfers between devices, on_device(): lax.all_to_all(outgoing.reshape(REPS * domains, 1, -1), ('rep', 'dom'), 0...  66.5 us
    pallas_call x1, Pallas kernels, local_pass(): pl.pallas_call(functools.partial(local_kernel, capacity), out_shape=(jax....  31.9 us
    all_to_all x1, blocking collectives, on_device(): lax.all_to_all(own_grads.reshape(domains, share, width), 'dom', 0, 0, til...  18.8 us
    all_to_all x1, blocking collectives, on_device(): lax.all_to_all(jnp.broadcast_to(total[None], (domains, share, width)), 'd...  17.7 us
    all_to_all x1, blocking collectives, on_device(): lax.all_to_all(jnp.broadcast_to(whole[None], (REPS, width, width)), 'rep'...  17.3 us
    all_to_all x1, starting transfers between devices, on_device(): lax.all_to_all(outgoing.reshape(REPS * domains, 1, -1), ('rep', 'dom'), 0...  15.7 us
    unnamed x27, local copies, waits for them, and re-layouts  13.2 us
    pallas_call x1, Pallas kernels, add_rows(): pl.pallas_call(functools.partial(add_kernel, capacity), out_shape=jax.Sha...  11 us
  transfers between devices with their start and end apart: 3, of which 1 were waited for; matrix products, arithmetic and copies ran while one was open for 1% of the time, Pallas kernels for 5%

profile of v1, /device:TPU:1, one launch (start us, length us, event | category | flops | bytes accessed | tf_op | source)
XLA Modules:
  0.0 210.2 jit_solution(9700695517570244102)
XLA Ops:
  7.2 0.0 copy-start
  7.2 1.6 copy-done
  8.8 0.9 copy-done.3
  9.7 0.9 copy-done.4
  10.6 0.9 copy-done.5
  11.5 0.9 copy-done.6
  12.4 0.7 copy-done.7
  13.1 0.8 copy-done.8
  13.9 0.8 copy-done.9
  14.8 0.7 copy-done.10
  15.5 0.7 copy-done.11
  16.2 0.7 copy-done.12
  16.9 31.9 %local_pass.1 = (f32[5376,128]{1,0:T(8,128)}, f32[1024,256]{1,0:T(8,128)S(1)}) custom-call(bf16[4096,256]{1,0:T(8,128)(2,1)S(1)} %copy-done, s32[15,1024]{1,0:T(8,128)S(1)} %bitcast.7, s32[10,128]{1,0:T(8,128)S(1)} %bitcast.8, s32[1,4096]{1,0:T(1,128)S(1)} %copy-done.7, s32[1,4096]{1,0:T(1,128)S(1)} %copy-done.7, s32[1,2048]{1,0:T(1,128)S(1)} %bitcast.9, ...), custom_call_target="tpu_custom_call" | custom-call | tf_op jit(solution)/shard_map/local_pass/pallas_call | solution.py:314
  48.7 1.0 copy-done.2
  49.7 15.7 %all-to-all-start = ((f32[256,1,2688]{2,1,0:T(1,128)}), f32[256,1,2688]{2,1,0:T(1,128)S(1)}, u32[]{:S(2)}, u32[]{:S(2)}) async-start(f32[256,1,2688]{2,1,0:T(1,128)} %bitcast.11), calls=%async_computation | async-start | bytes 5505024 | tf_op jit(solution)/shard_map/all_to_all | solution.py:396
  65.4 0.0 reduce-scatter.2.cloned.1.call-start
  65.4 0.7 reduce-scatter.2.cloned.1.call-update
  66.1 0.0 all-gather.2.cloned.1.call-start
  66.2 66.5 %all-to-all-done = f32[256,1,2688]{2,1,0:T(1,128)S(1)} async-done(((f32[256,1,2688]{2,1,0:T(1,128)}), f32[256,1,2688]{2,1,0:T(1,128)S(1)}, u32[]{:S(2)}, u32[]{:S(2)}) %all-to-all-start) | async-done | bytes 2752544 | tf_op jit(solution)/shard_map/all_to_all | solution.py:396
  132.7 11.0 %add_rows.1 = f32[512,256]{1,0:T(8,128)} custom-call(f32[5376,128]{1,0:T(8,128)S(1)} %bitcast.6), custom_call_target="tpu_custom_call" | custom-call | tf_op jit(solution)/shard_map/add_rows/pallas_call | solution.py:341
  143.7 0.0 all-gather.2.cloned.1.call-update
  143.7 0.0 reduce-scatter.2.cloned.1.call-done
  143.7 1.0 reshape.19
  144.7 18.8 %all_to_all.20 = f32[64,4,256]{2,1,0:T(4,128)S(1)} all-to-all(f32[64,4,256]{2,1,0:T(4,128)S(1)} %reshape.19), channel_id=1, replica_groups=mesh['dom'=64,'rep'=4] {'dom'}, dimensions={0} | all-to-all | bytes 524288 | tf_op jit(solution)/shard_map/all_to_all | solution.py:401
  163.5 0.1 reduce_sum.9
  163.7 17.7 %all_to_all.21 = f32[64,4,256]{2,1,0:T(4,128)S(1)} all-to-all(f32[64,4,256]{2,1,0:T(4,128)S(1)} %broadcast_in_dim.17), channel_id=1, replica_groups=mesh['dom'=64,'rep'=4] {'dom'}, dimensions={0} | all-to-all | bytes 524288 | tf_op jit(solution)/shard_map/all_to_all | solution.py:403
  181.3 0.1 broadcast_in_dim.18
  181.4 0.1 broadcast_in_dim.19
  181.5 17.3 %all_to_all.22 = f32[4,256,256]{2,1,0:T(8,128)S(1)} all-to-all(f32[4,256,256]{2,1,0:T(8,128)S(1)} %broadcast_in_dim.19), channel_id=1, replica_groups=mesh['dom'=64,'rep'=4] {'rep'}, dimensions={0} | all-to-all | bytes 2097152 | tf_op jit(solution)/shard_map/all_to_all | solution.py:406
  198.9 1.6 copy-done.1
  200.5 1.9 join_columns.1
  202.4 1.0 copy.15
  (15 shorter events, 0.1 us)
Async XLA Ops:
  7.2 1.6 copy-start
  8.8 0.9 copy-start.3
  9.7 0.9 copy-start.4
  10.6 0.9 copy-start.5
  11.5 0.9 copy-start.6
  12.4 0.7 copy-start.7
  13.1 0.8 copy-start.8
  13.9 0.8 copy-start.9
  14.8 0.7 copy-start.10
  15.5 0.7 copy-start.11
  16.2 0.7 copy-start.12
  48.7 1.0 copy-start.2
  49.7 83.0 %all-to-all-start = ((f32[256,1,2688]{2,1,0:T(1,128)}), f32[256,1,2688]{2,1,0:T(1,128)S(1)}, u32[]{:S(2)}, u32[]{:S(2)}) async-start(f32[256,1,2688]{2,1,0:T(1,128)} %bitcast.11), calls=%async_computation | async-start | bytes 5505024 | tf_op jit(solution)/shard_map/all_to_all | solution.py:396
  65.4 78.3 %reduce-scatter.2.cloned.1.call-start = ((), (), s32[]{:S(2)}) async-start(), calls=%async_computation.6 | async-start | bytes 1310720 | tf_op jit(solution)/shard_map/reduce_scatter | solution.py:399
  66.1 132.8 %all-gather.2.cloned.1.call-start = ((), (), s32[]{:S(2)}) async-start(), calls=%async_computation.5 | async-start | bytes 2621440 | tf_op jit(solution)/shard_map/all_gather | solution.py:410
  198.9 1.6 copy-start.1
Sparse Core Ops, SparseCore 0:
  69.3 32.8 reduce-scatter.1
  143.8 27.9 all-gather.1

commit v2 on v1

--- a/solution.py
+++ b/solution.py
@@ -10,6 +10,8 @@
 ROWS_OWN = 2048
 GRAD_SCALE = 16.0
 NIBBLES = 8
+DEPTH = 256
+GROUP = 32
 NIBBLE_BITS = 4
 SPAN = 256
 LANES = 128
@@ -30,18 +32,17 @@
 
 def local_kernel(
     capacity,
-    x_ref,
-    first_ref,
-    second_ref,
-    ids_ref,
-    ids_smem,
-    owners_ref,
-    rows_ref,
-    cot_ref,
-    self1_ref,
-    agg1_ref,
-    self2_ref,
-    agg2_ref,
+    x_hbm,
+    first_hbm,
+    second_hbm,
+    ids_hbm,
+    owners_hbm,
+    rows_hbm,
+    cot_hbm,
+    self1_hbm,
+    agg1_hbm,
+    self2_hbm,
+    agg2_hbm,
     out_ref,
     grads_ref,
     xt_ref,
@@ -55,7 +56,41 @@
     target_ref,
     high_ref,
     low_ref,
+    x_ref,
+    first_ref,
+    second_ref,
+    ids_ref,
+    owners_ref,
+    rows_ref,
+    cot_ref,
+    self1_ref,
+    agg1_ref,
+    self2_ref,
+    agg2_ref,
+    ids_smem,
+    sems,
 ):
+    sources = (
+        (owners_hbm, owners_ref),
+        (rows_hbm, rows_ref),
+        (first_hbm, first_ref),
+        (x_hbm, x_ref),
+        (second_hbm, second_ref),
+        (cot_hbm, cot_ref),
+        (self1_hbm, self1_ref),
+        (agg1_hbm, agg1_ref),
+        (self2_hbm, self2_ref),
+        (agg2_hbm, agg2_ref),
+        (ids_hbm, ids_ref),
+        (ids_hbm, ids_smem),
+    )
+    copies = [
+        pltpu.make_async_copy(source, local, sems.at[n])
+        for n, (source, local) in enumerate(sources)
+    ]
+    for copy in copies:
+        copy.start()
+
     inputs, width = x_ref.shape
     fan1, firsts = first_ref.shape
     fan2, batch = second_ref.shape
@@ -63,107 +98,11 @@
     domains = high_ref.shape[0]
     words = inputs // NIBBLES
     lanes = 128
-    depth = 64
-
-    eye = (
-        lax.broadcasted_iota(jnp.int32, (width, width), 0)
-        == lax.broadcasted_iota(jnp.int32, (width, width), 1)
-    ).astype(BF16)
-
-    def turn(c, _):
-        at = pl.multiple_of(c * 512, 512)
-        xt_ref[:, pl.ds(at, 512)] = matmul(eye, x_ref[pl.ds(at, 512), :], NT).astype(BF16)
-        return 0
-
-    lax.fori_loop(0, inputs // 512, turn, 0)
-
-    def count(step, _):
-        col = pl.multiple_of((step // (words // depth)) * lanes, lanes)
-        row = pl.multiple_of((step % (words // depth)) * depth, depth)
-        nodes = first_ref[:, pl.ds(col, lanes)]
-        keys = nodes % words
-        values = jnp.left_shift(jnp.int32(1), (nodes // words) * NIBBLE_BITS)
-        place = lax.broadcasted_iota(jnp.int32, (depth, lanes), 0) + row
-        total = jnp.zeros((depth, lanes), jnp.int32)
-        for k in range(fan1):
-            total = total + jnp.where(keys[k : k + 1, :] == place, values[k : k + 1, :], 0)
-        for part in range(NIBBLES):
-            counts = jnp.bitwise_and(jnp.right_shift(total, part * NIBBLE_BITS), 15)
-            table_ref[pl.ds(part * words + row, depth), pl.ds(col, lanes)] = counts.astype(
-                F32
-            ).astype(BF16)
-        return 0
-
-    lax.fori_loop(0, (firsts // lanes) * (words // depth), count, 0)
-
-    def mean(c, _):
-        at = pl.multiple_of(c * SPAN, SPAN)
-        mean_ref[:, pl.ds(at, SPAN)] = (
-            matmul(xt_ref[...], table_ref[:, pl.ds(at, SPAN)]) / fan1
-        ).astype(BF16)
-        return 0
-
-    lax.fori_loop(0, firsts // SPAN, mean, 0)
-
-    mean_one = mean_ref[...]
-    selfs = xt_ref[:, :firsts]
-    contract_first = (((0,), (0,)), ((), ()))
-    preact = matmul(self1_ref[...], selfs, contract_first) + matmul(
-        agg1_ref[...], mean_one, contract_first
-    )
-    gate = sigmoid(preact)
-    hidden = (preact * gate).astype(BF16)
-    second = jnp.zeros((firsts, batch), F32)
-    place2 = lax.broadcasted_iota(jnp.int32, (firsts, batch), 0)
-    for k in range(fan2):
-        second = second + (second_ref[k : k + 1, :] == place2).astype(F32)
-    second = second.astype(BF16)
-    mean_two = (matmul(hidden, second) / fan2).astype(BF16)
-    cot = cot_ref[...]
-    grads_ref[2 * width : 3 * width, :] = matmul(hidden[:, :batch], cot)
-    grads_ref[3 * width :, :] = matmul(mean_two, cot)
-    down_two = (matmul(agg2_ref[...], cot, NT) / fan2).astype(BF16)
-    hidden_grad = matmul(down_two, second, NT)
-    targets_grad = hidden_grad[:, :batch] + matmul(self2_ref[...], cot, NT)
-    hidden_grad = jnp.concatenate([targets_grad, hidden_grad[:, batch:]], axis=1)
-    pre_grad = (hidden_grad * (gate * (1.0 + preact * (1.0 - gate)))).astype(BF16)
-    grads_ref[:width, :] = matmul(selfs, pre_grad, NT)
-    grads_ref[width : 2 * width, :] = matmul(mean_one, pre_grad, NT)
-    down_ref[...] = (matmul(agg1_ref[...], pre_grad) / fan1).astype(BF16)
-    selfgrad_ref[...] = matmul(self1_ref[...], pre_grad)
-
-    step_rows = 512
-    for c in range(firsts // step_rows):
-        at = c * step_rows
-        spread_ref[:, at : at + step_rows] = (
-            matmul(down_ref[...], table_ref[at : at + step_rows, :], NT)
-            + selfgrad_ref[:, at : at + step_rows]
-        ).astype(BF16)
-
-    def spread(c, _):
-        at = pl.multiple_of(c * step_rows, step_rows)
-        spread_ref[:, pl.ds(at, step_rows)] = matmul(
-            down_ref[...], table_ref[pl.ds(at, step_rows), :], NT
-        ).astype(BF16)
-        return 0
-
-    lax.fori_loop(firsts // step_rows, inputs // step_rows, spread, 0)
-
-    window = SPAN + 8
-    merged_ref[...] = jnp.zeros(merged_ref.shape, F32)
-
-    def merge(c, _):
-        at = pl.multiple_of(c * SPAN, SPAN)
-        low = jnp.minimum(ids_smem[0, at] // 8, (uniq - window) // 8) * 8
-        low = pl.multiple_of(low, 8)
-        place = lax.broadcasted_iota(jnp.int32, (window, SPAN), 0) + low
-        picker = (ids_ref[:, pl.ds(at, SPAN)] == place).astype(F32).astype(BF16)
-        merged_ref[pl.ds(low, window), :] += matmul(picker, spread_ref[:, pl.ds(at, SPAN)], NT)
-        return 0
-
-    lax.fori_loop(0, inputs // SPAN, merge, 0)
-    picked_ref[...] = (merged_ref[...] * GRAD_SCALE).astype(BF16)
-
+    depth = DEPTH
+    turned = inputs // ((firsts // lanes) * (words // depth))
+
+    copies[0].wait()
+    copies[1].wait()
     upper = (
         lax.broadcasted_iota(jnp.int32, (SPAN, SPAN), 0)
         < lax.broadcasted_iota(jnp.int32, (SPAN, SPAN), 1)
@@ -193,7 +132,106 @@
     high_ref[...] = high
     low_ref[...] = low
 
-    group = 8
+    eye = (
+        lax.broadcasted_iota(jnp.int32, (width, width), 0)
+        == lax.broadcasted_iota(jnp.int32, (width, width), 1)
+    ).astype(BF16)
+
+    copies[2].wait()
+    copies[3].wait()
+
+    def count(step, _):
+        col = pl.multiple_of((step // (words // depth)) * lanes, lanes)
+        row = pl.multiple_of((step % (words // depth)) * depth, depth)
+        nodes = first_ref[:, pl.ds(col, lanes)]
+        keys = nodes % words
+        values = jnp.left_shift(jnp.int32(1), (nodes // words) * NIBBLE_BITS)
+        place = lax.broadcasted_iota(jnp.int32, (depth, lanes), 0) + row
+        total = jnp.zeros((depth, lanes), jnp.int32)
+        for k in range(fan1):
+            total = total + jnp.where(keys[k : k + 1, :] == place, values[k : k + 1, :], 0)
+        for part in range(NIBBLES):
+            counts = jnp.bitwise_and(jnp.right_shift(total, part * NIBBLE_BITS), 15)
+            table_ref[pl.ds(part * words + row, depth), pl.ds(col, lanes)] = counts.astype(
+                F32
+            ).astype(BF16)
+        at = pl.multiple_of(step * turned, turned)
+        xt_ref[:, pl.ds(at, turned)] = matmul(eye, x_ref[pl.ds(at, turned), :], NT).astype(BF16)
+        return 0
+
+    lax.fori_loop(0, (firsts // lanes) * (words // depth), count, 0, unroll=2)
+
+    def mean(c, _):
+        at = pl.multiple_of(c * SPAN, SPAN)
+        mean_ref[:, pl.ds(at, SPAN)] = (
+            matmul(xt_ref[...], table_ref[:, pl.ds(at, SPAN)]) / fan1
+        ).astype(BF16)
+        return 0
+
+    lax.fori_loop(0, firsts // SPAN, mean, 0, unroll=2)
+
+    for copy in copies[4:]:
+        copy.wait()
+    mean_one = mean_ref[...]
+    selfs = xt_ref[:, :firsts]
+    contract_first = (((0,), (0,)), ((), ()))
+    preact = matmul(self1_ref[...], selfs, contract_first) + matmul(
+        agg1_ref[...], mean_one, contract_first
+    )
+    gate = sigmoid(preact)
+    hidden = (preact * gate).astype(BF16)
+    second = jnp.zeros((firsts, batch), F32)
+    place2 = lax.broadcasted_iota(jnp.int32, (firsts, batch), 0)
+    for k in range(fan2):
+        second = second + (second_ref[k : k + 1, :] == place2).astype(F32)
+    second = second.astype(BF16)
+    mean_two = (matmul(hidden, second) / fan2).astype(BF16)
+    cot = cot_ref[...]
+    grads_ref[2 * width : 3 * width, :] = matmul(hidden[:, :batch], cot)
+    grads_ref[3 * width :, :] = matmul(mean_two, cot)
+    down_two = (matmul(agg2_ref[...], cot, NT) / fan2).astype(BF16)
+    hidden_grad = matmul(down_two, second, NT)
+    targets_grad = hidden_grad[:, :batch] + matmul(self2_ref[...], cot, NT)
+    hidden_grad = jnp.concatenate([targets_grad, hidden_grad[:, batch:]], axis=1)
+    pre_grad = (hidden_grad * (gate * (1.0 + preact * (1.0 - gate)))).astype(BF16)
+    grads_ref[:width, :] = matmul(selfs, pre_grad, NT)
+    grads_ref[width : 2 * width, :] = matmul(mean_one, pre_grad, NT)
+    down_ref[...] = (matmul(agg1_ref[...], pre_grad) / fan1).astype(BF16)
+    selfgrad_ref[...] = matmul(self1_ref[...], pre_grad)
+
+    step_rows = 512
+    for c in range(firsts // step_rows):
+        at = c * step_rows
+        spread_ref[:, at : at + step_rows] = (
+            matmul(down_ref[...], table_ref[at : at + step_rows, :], NT)
+            + selfgrad_ref[:, at : at + step_rows]
+        ).astype(BF16)
+
+    def spread(c, _):
+        at = pl.multiple_of(c * step_rows, step_rows)
+        spread_ref[:, pl.ds(at, step_rows)] = matmul(
+            down_ref[...], table_ref[pl.ds(at, step_rows), :], NT
+        ).astype(BF16)
+        return 0
+
+    lax.fori_loop(firsts // step_rows, inputs // step_rows, spread, 0, unroll=2)
+
+    window = SPAN + 8
+    merged_ref[...] = jnp.zeros(merged_ref.shape, F32)
+
+    def merge(c, _):
+        at = pl.multiple_of(c * SPAN, SPAN)
+        low = jnp.minimum(ids_smem[0, at] // 8, (uniq - window) // 8) * 8
+        low = pl.multiple_of(low, 8)
+        place = lax.broadcasted_iota(jnp.int32, (window, SPAN), 0) + low
+        picker = (ids_ref[:, pl.ds(at, SPAN)] == place).astype(F32).astype(BF16)
+        merged_ref[pl.ds(low, window), :] += matmul(picker, spread_ref[:, pl.ds(at, SPAN)], NT)
+        return 0
+
+    lax.fori_loop(0, inputs // SPAN, merge, 0, unroll=4)
+    picked_ref[...] = (merged_ref[...] * GRAD_SCALE).astype(BF16)
+
+    group = GROUP
     chunk = group * tall
     quarter = width // REPS
     label_line = (
@@ -226,7 +264,7 @@
 def add_kernel(capacity, lines_ref, table_ref):
     half = capacity // 2
     tall = half + 1
-    group = 32
+    group = 64
     chunk = group * tall
     sources = lines_ref.shape[0] // tall
     quarter = LANES // 2
@@ -303,21 +341,23 @@
 
 
 VMEM = pl.BlockSpec(memory_space=pltpu.VMEM)
-SMEM = pl.BlockSpec(memory_space=pltpu.SMEM)
+HBM = pl.BlockSpec(memory_space=pltpu.HBM)
 PARAMS = pltpu.CompilerParams(vmem_limit_bytes=48 * 1024 * 1024)
+LOCAL_PARAMS = pltpu.CompilerParams(vmem_limit_bytes=60 * 1024 * 1024)
 
 
 def local_pass(capacity, domains, x, first, second, ids, owners, rows, cot, self1, agg1, self2, agg2):
     inputs, width = x.shape
     firsts = first.shape[1]
     uniq = owners.shape[1]
+    arrays = (x, first, second, ids, owners, rows, cot, self1, agg1, self2, agg2)
     return pl.pallas_call(
         functools.partial(local_kernel, capacity),
         out_shape=(
             jax.ShapeDtypeStruct((REPS * domains * (capacity // 2 + 1), LANES), F32),
             jax.ShapeDtypeStruct((4 * width, width), F32),
         ),
-        in_specs=[VMEM] * 4 + [SMEM] + [VMEM] * 7,
+        in_specs=[HBM] * 11,
         out_specs=(VMEM, VMEM),
         scratch_shapes=[
             pltpu.VMEM((width, inputs), BF16),
@@ -331,10 +371,13 @@
             pltpu.VMEM((2, uniq), jnp.int32),
             pltpu.VMEM((domains, LANES), F32),
             pltpu.VMEM((domains, LANES), F32),
+            *[pltpu.VMEM(a.shape, a.dtype) for a in arrays],
+            pltpu.SMEM(ids.shape, ids.dtype),
+            pltpu.SemaphoreType.DMA((len(arrays) + 1,)),
         ],
-        compiler_params=PARAMS,
+        compiler_params=LOCAL_PARAMS,
         name="local_pass",
-    )(x, first, second, ids, ids, owners, rows, cot, self1, agg1, self2, agg2)
+    )(*arrays)
 
 
 def add_rows(capacity, lines):
@@ -403,6 +446,7 @@
     whole = lax.all_to_all(
         jnp.broadcast_to(total[None], (domains, share, width)), "dom", 0, 0, tiled=True
     ).reshape(width, width)
+    arrived, whole = lax.optimization_barrier((arrived, whole))
     weight_grads = lax.all_to_all(
         jnp.broadcast_to(whole[None], (REPS, width, width)), "rep", 0, 0, tiled=True
     )

time: 211 us -> 234 us (1.11)
  waiting for transfers between devices: 67.2 us -> 109 us
  blocking collectives: 53.8 us -> 64.5 us
  local copies, waits for them, and re-layouts: 14.4 us -> 3.79 us
  starting transfers between devices: 15.7 us -> 5.9 us
  Pallas kernels: 44.8 us -> 36.6 us
    reduce_scatter x1, waiting for transfers between devices: 0.02 us -> 28.7 us  [on_device(): own_grads = lax.psum_scatter(grads, 'rep', scatter_dimension=0, tiled=True)]
    all_gather x1, waiting for transfers between devices: 0.01 us -> 13.1 us  [on_device(): table = join_columns(lax.all_gather(quarter, 'rep', axis=0, tiled=True))]
    unnamed x27 -> x3, local copies, waits for them, and re-layouts: 13.2 us -> 2.56 us
    all_to_all x1, starting transfers between devices: 15.7 us -> 5.64 us  [on_device(): lax.all_to_all(outgoing.reshape(REPS * domains, 1, -1), ('rep', 'dom'), 0...]
    pallas_call x1, Pallas kernels: 31.9 us -> 24.6 us  [local_pass(): pl.pallas_call(functools.partial(local_kernel, capacity), out_shape=(jax....]
    all_to_all x1, blocking collectives: 18.8 us -> 25 us  [on_device(): lax.all_to_all(own_grads.reshape(domains, share, width), 'dom', 0, 0, til...]
    all_to_all x1, blocking collectives: 17.3 us -> 21.8 us  [on_device(): lax.all_to_all(jnp.broadcast_to(whole[None], (REPS, width, width)), 'rep'...]
  transfers between devices with their start and end apart: 3 -> 3, of which waited for: 1 -> 3; matrix products, arithmetic and copies ran while one was open for 1% -> 0% of each run, Pallas kernels for 5% -> 0%
where the time goes in v2:
time: 234 us
  waiting for transfers between devices  109 us (47%)
  blocking collectives  64.5 us (28%)
  Pallas kernels  36.6 us (16%)
  between operations  14.1 us (6%)
  starting transfers between devices  5.9 us (3%)
  local copies, waits for them, and re-layouts  3.79 us (2%)
    all_to_all x1, waiting for transfers between devices, on_device(): lax.all_to_all(outgoing.reshape(REPS * domains, 1, -1), ('rep', 'dom'), 0...  67 us
    reduce_scatter x1, waiting for transfers between devices, on_device(): own_grads = lax.psum_scatter(grads, 'rep', scatter_dimension=0, tiled=True)  28.7 us
    all_to_all x1, blocking collectives, on_device(): lax.all_to_all(own_grads.reshape(domains, share, width), 'dom', 0, 0, til...  25 us
    pallas_call x1, Pallas kernels, local_pass(): pl.pallas_call(functools.partial(local_kernel, capacity), out_shape=(jax....  24.6 us
    all_to_all x1, blocking collectives, on_device(): lax.all_to_all(jnp.broadcast_to(whole[None], (REPS, width, width)), 'rep'...  21.8 us
    all_to_all x1, blocking collectives, on_device(): lax.all_to_all(jnp.broadcast_to(total[None], (domains, share, width)), 'd...  17.7 us
    all_gather x1, waiting for transfers between devices, on_device(): table = join_columns(lax.all_gather(quarter, 'rep', axis=0, tiled=True))  13.1 us
    pallas_call x1, Pallas kernels, add_rows(): pl.pallas_call(functools.partial(add_kernel, capacity), out_shape=jax.Sha...  10 us
  transfers between devices with their start and end apart: 3, of which 3 were waited for; matrix products, arithmetic and copies ran while one was open for 0% of the time, Pallas kernels for 0%

profile of v2, /device:TPU:1, one launch (start us, length us, event | category | flops | bytes accessed | tf_op | source)
XLA Modules:
  0.0 233.8 jit_solution(10710526303683892776)
XLA Ops:
  7.2 0.0 reduce-scatter.2.cloned.1.call-start
  7.2 24.6 %local_pass.1 = (f32[5376,128]{1,0:T(8,128)}, f32[1024,256]{1,0:T(8,128)}) custom-call(bf16[4096,256]{1,0:T(8,128)(2,1)} %x_hbm.1, s32[15,1024]{1,0:T(8,128)} %bitcast.8, s32[10,128]{1,0:T(8,128)} %bitcast.9, s32[1,4096]{1,0:T(1,128)} %ids_hbm.1, s32[1,2048]{1,0:T(1,128)} %bitcast.10, s32[1,2048]{1,0:T(1,128)} %bitcast.11, bf16[128,256]{1,0:T(8,128)(2,1)} %cot_hbm.1, ...), custom_call_target="tpu_custom_call" | custom-call | tf_op jit(solution)/shard_map/local_pass/pallas_call | solution.py:354
  31.8 0.0 reduce-scatter.2.cloned.1.call-update
  31.9 28.7 %reduce-scatter.2.cloned.1.call-done = f32[256,256]{1,0:T(8,128)} async-done(((f32[1024,256]{1,0:T(8,128)}), f32[256,256]{1,0:T(8,128)}) %reduce-scatter.2.cloned.1.call-update) | async-done | bytes 262160 | tf_op jit(solution)/shard_map/reduce_scatter | solution.py:442
  60.6 1.0 reshape.21
  61.6 25.0 %all_to_all.20 = f32[64,4,256]{2,1,0:T(4,128)S(1)} all-to-all(f32[64,4,256]{2,1,0:T(4,128)S(1)} %reshape.21), channel_id=1, replica_groups=mesh['dom'=64,'rep'=4] {'dom'}, dimensions={0} | all-to-all | bytes 524288 | tf_op jit(solution)/shard_map/all_to_all | solution.py:444
  86.6 0.1 reduce_sum.9
  86.7 17.7 %all_to_all.21 = f32[64,4,256]{2,1,0:T(4,128)S(1)} all-to-all(f32[64,4,256]{2,1,0:T(4,128)S(1)} %broadcast_in_dim.7), channel_id=1, replica_groups=mesh['dom'=64,'rep'=4] {'dom'}, dimensions={0} | all-to-all | bytes 524288 | tf_op jit(solution)/shard_map/all_to_all | solution.py:446
  104.4 5.6 %all-to-all-start = ((f32[256,1,2688]{2,1,0:T(1,128)}), f32[256,1,2688]{2,1,0:T(1,128)S(1)}, u32[]{:S(2)}, u32[]{:S(2)}) async-start(f32[256,1,2688]{2,1,0:T(1,128)} %bitcast.7), calls=%async_computation | async-start | bytes 5505024 | tf_op jit(solution)/shard_map/all_to_all | solution.py:439
  110.0 0.2 all-gather.2.cloned.1.call-start
  110.3 0.1 reshape.22
  110.4 67.0 %all-to-all-done = f32[256,1,2688]{2,1,0:T(1,128)S(1)} async-done(((f32[256,1,2688]{2,1,0:T(1,128)}), f32[256,1,2688]{2,1,0:T(1,128)S(1)}, u32[]{:S(2)}, u32[]{:S(2)}) %all-to-all-start) | async-done | bytes 2752544 | tf_op jit(solution)/shard_map/all_to_all | solution.py:439
  177.3 10.0 %add_rows.1 = f32[512,256]{1,0:T(8,128)} custom-call(f32[5376,128]{1,0:T(8,128)S(1)} %bitcast.6), custom_call_target="tpu_custom_call" | custom-call | tf_op jit(solution)/shard_map/add_rows/pallas_call | solution.py:384
  187.4 0.0 all-gather.2.cloned.1.call-update
  187.4 0.1 broadcast_in_dim.8
  187.5 21.8 %all_to_all.22 = f32[4,256,256]{2,1,0:T(8,128)S(1)} all-to-all(f32[4,256,256]{2,1,0:T(8,128)S(1)} %broadcast_in_dim.8), channel_id=1, replica_groups=mesh['dom'=64,'rep'=4] {'rep'}, dimensions={0} | all-to-all | bytes 2097152 | tf_op jit(solution)/shard_map/all_to_all | solution.py:450
  209.3 13.1 %all-gather.2.cloned.1.call-done.parts_ref = f32[2048,256]{1,0:T(8,128)} async-done(((f32[512,256]{1,0:T(8,128)}), f32[2048,256]{1,0:T(8,128)}) %all-gather.2.cloned.1.call-update) | async-done | bytes 2097168 | tf_op jit(solution)/shard_map/all_gather | solution.py:454
  222.4 0.0 copy-start
  222.4 1.6 copy-done
  224.0 1.9 join_columns.1
  226.0 1.0 copy.15
  (2 shorter events, 0.0 us)
Async XLA Ops:
  7.2 53.4 %reduce-scatter.2.cloned.1.call-start = ((), (), s32[]{:S(2)}) async-start(), calls=%async_computation.5 | async-start | bytes 1310720 | tf_op jit(solution)/shard_map/reduce_scatter | solution.py:442
  104.4 73.0 %all-to-all-start = ((f32[256,1,2688]{2,1,0:T(1,128)}), f32[256,1,2688]{2,1,0:T(1,128)S(1)}, u32[]{:S(2)}, u32[]{:S(2)}) async-start(f32[256,1,2688]{2,1,0:T(1,128)} %bitcast.7), calls=%async_computation | async-start | bytes 5505024 | tf_op jit(solution)/shard_map/all_to_all | solution.py:439
  110.0 112.4 %all-gather.2.cloned.1.call-start = ((), (), s32[]{:S(2)}) async-start(), calls=%async_computation.6 | async-start | bytes 2621440 | tf_op jit(solution)/shard_map/all_gather | solution.py:454
  222.4 1.6 copy-start
Sparse Core Ops, SparseCore 0:
  32.0 28.5 reduce-scatter.1
  187.5 34.8 all-gather.1

commit v3 on v2

--- a/solution.py
+++ b/solution.py
@@ -402,6 +402,22 @@
     )(parts)
 
 
+def sum_over_domains(value, domains):
+    place = lax.axis_index("dom")
+    steps = [1 << bit for bit in range(domains.bit_length() - 1)]
+
+    def swap(part, step):
+        return lax.ppermute(part, "dom", [(i, i ^ step) for i in range(domains)])
+
+    for step in steps:
+        pairs = value.reshape(value.shape[0] // 2, 2, *value.shape[1:])
+        upper = (place & step) != 0
+        sent = jnp.where(upper, pairs[:, 0], pairs[:, 1])
+        kept = jnp.where(upper, pairs[:, 1], pairs[:, 0])
+        value = kept + swap(sent, step)
+    return value[0]
+
+
 def on_device(
     node_input,
     neighbor_first,
@@ -441,12 +457,11 @@
     )
     own_grads = lax.psum_scatter(grads, "rep", scatter_dimension=0, tiled=True)
     share = width // domains
-    shares = lax.all_to_all(own_grads.reshape(domains, share, width), "dom", 0, 0, tiled=True)
-    total = jnp.sum(shares, axis=0) * factor
+    total = sum_over_domains(own_grads.reshape(domains, share, width), domains) * factor
+    arrived, total = lax.optimization_barrier((arrived, total))
     whole = lax.all_to_all(
         jnp.broadcast_to(total[None], (domains, share, width)), "dom", 0, 0, tiled=True
     ).reshape(width, width)
-    arrived, whole = lax.optimization_barrier((arrived, whole))
     weight_grads = lax.all_to_all(
         jnp.broadcast_to(whole[None], (REPS, width, width)), "rep", 0, 0, tiled=True
     )

time: 234 us -> 188 us (0.80)
  waiting for transfers between devices: 109 us -> 57.9 us
  starting transfers between devices: 5.9 us -> 26.9 us
  blocking collectives: 64.5 us -> 47.7 us
    all_to_all x1, waiting for transfers between devices: 67 us -> 0.01 us  [on_device(): lax.all_to_all(outgoing.reshape(REPS * domains, 1, -1), ('rep', 'dom'), 0...]
    all_to_all x1 -> x0, blocking collectives: 25 us -> none  [on_device(): lax.all_to_all(own_grads.reshape(domains, share, width), 'dom', 0, 0, til...]
    ppermute x0 -> x6, waiting for transfers between devices: none -> 21.1 us  [swap(): return lax.ppermute(part, 'dom', [(i, i ^ step) for i in range(domains)])]
    all_gather x1, waiting for transfers between devices: 13.1 us -> 0.01 us  [on_device(): table = join_columns(lax.all_gather(quarter, 'rep', axis=0, tiled=True))]
    ppermute x0 -> x6, starting transfers between devices: none -> 11.2 us  [swap(): return lax.ppermute(part, 'dom', [(i, i ^ step) for i in range(domains)])]
    all_to_all x1, starting transfers between devices: 5.64 us -> 15.7 us  [on_device(): lax.all_to_all(outgoing.reshape(REPS * domains, 1, -1), ('rep', 'dom'), 0...]
    all_to_all x1, blocking collectives: 17.7 us -> 25.7 us  [on_device(): lax.all_to_all(jnp.broadcast_to(total[None], (domains, share, width)), 'd...]
    reduce_scatter x1, waiting for transfers between devices: 28.7 us -> 36.1 us  [on_device(): own_grads = lax.psum_scatter(grads, 'rep', scatter_dimension=0, tiled=True)]
  transfers between devices with their start and end apart: 3 -> 9, of which waited for: 3 -> 7; matrix products, arithmetic and copies ran while one was open for 0% -> 1% of each run, Pallas kernels for 0% -> 0%
where the time goes in v3:
time: 188 us; the launch traced here: 187 us
  waiting for transfers between devices  57.9 us (31%)
  blocking collectives  47.7 us (25%)
  Pallas kernels  36.5 us (19%)
  starting transfers between devices  26.9 us (14%)
  between operations  14.1 us (8%)
  local copies, waits for them, and re-layouts  3.79 us (2%)
    reduce_scatter x1, waiting for transfers between devices, on_device(): own_grads = lax.psum_scatter(grads, 'rep', scatter_dimension=0, tiled=True)  36.1 us
    all_to_all x1, blocking collectives, on_device(): lax.all_to_all(jnp.broadcast_to(total[None], (domains, share, width)), 'd...  25.7 us
    pallas_call x1, Pallas kernels, local_pass(): pl.pallas_call(functools.partial(local_kernel, capacity), out_shape=(jax....  24.6 us
    all_to_all x1, blocking collectives, on_device(): lax.all_to_all(jnp.broadcast_to(whole[None], (REPS, width, width)), 'rep'...  22 us
    ppermute x6, waiting for transfers between devices, swap(): return lax.ppermute(part, 'dom', [(i, i ^ step) for i in range(domains)])  21.1 us
    all_to_all x1, starting transfers between devices, on_device(): lax.all_to_all(outgoing.reshape(REPS * domains, 1, -1), ('rep', 'dom'), 0...  15.7 us
    ppermute x6, starting transfers between devices, swap(): return lax.ppermute(part, 'dom', [(i, i ^ step) for i in range(domains)])  11.2 us
    pallas_call x1, Pallas kernels, add_rows(): pl.pallas_call(functools.partial(add_kernel, capacity), out_shape=jax.Sha...  10 us
  transfers between devices with their start and end apart: 9, of which 7 were waited for; matrix products, arithmetic and copies ran while one was open for 1% of the time, Pallas kernels for 0%

profile of v3, /device:TPU:1, one launch (start us, length us, event | category | flops | bytes accessed | tf_op | source)
XLA Modules:
  0.0 187.2 jit_solution(8125028272655341566)
XLA Ops:
  7.2 24.6 %local_pass.1 = (f32[5376,128]{1,0:T(8,128)}, f32[1024,256]{1,0:T(8,128)}) custom-call(bf16[4096,256]{1,0:T(8,128)(2,1)} %x_hbm.1, s32[15,1024]{1,0:T(8,128)} %bitcast.124, s32[10,128]{1,0:T(8,128)} %bitcast.125, s32[1,4096]{1,0:T(1,128)} %ids_hbm.1, s32[1,2048]{1,0:T(1,128)} %bitcast.126, s32[1,2048]{1,0:T(1,128)} %bitcast.127, bf16[128,256]{1,0:T(8,128)(2,1)} %cot_hbm.1, ...), custom_call_target="tpu_custom_call" | custom-call | tf_op jit(solution)/shard_map/local_pass/pallas_call | solution.py:354
  31.8 15.7 %all-to-all-start = ((f32[256,1,2688]{2,1,0:T(1,128)}), f32[256,1,2688]{2,1,0:T(1,128)S(1)}, u32[]{:S(2)}, u32[]{:S(2)}) async-start(f32[256,1,2688]{2,1,0:T(1,128)} %bitcast.115), calls=%async_computation | async-start | bytes 5505024 | tf_op jit(solution)/shard_map/all_to_all | solution.py:455
  47.5 0.0 reduce-scatter.2.cloned.1.call-start
  47.5 0.7 reduce-scatter.2.cloned.1.call-update
  48.2 0.0 all-gather.2.cloned.1.call-start
  48.2 36.1 %reduce-scatter.2.cloned.1.call-done = f32[256,256]{1,0:T(8,128)} async-done(((f32[1024,256]{1,0:T(8,128)}), f32[256,256]{1,0:T(8,128)}) %reduce-scatter.2.cloned.1.call-update) | async-done | bytes 262160 | tf_op jit(solution)/shard_map/reduce_scatter | solution.py:458
  84.3 1.0 reshape_reshape.3
  85.4 0.5 collective-permute-start
  85.9 1.0 collective-permute-done
  86.9 0.8 collective-permute-start.1
  87.7 4.1 %collective-permute-done.1 = f32[16,4,256]{2,1,0:T(4,128)S(1)} collective-permute-done((f32[16,4,256]{2,1,0:T(4,128)S(1)}, f32[16,4,256]{2,1,0:T(4,128)S(1)}, u32[]{:S(2)}, u32[]{:S(2)}) %collective-permute-start.1) | collective-permute-done | bytes 65568 | tf_op jit(solution)/shard_map/ppermute | solution.py:410
  91.9 2.4 %collective-permute-start.2 = (f32[8,4,256]{2,1,0:T(4,128)S(1)}, f32[8,4,256]{2,1,0:T(4,128)S(1)}, u32[]{:S(2)}, u32[]{:S(2)}) collective-permute-start(f32[8,4,256]{2,1,0:T(4,128)S(1)} %select_bitcast_fusion.2), channel_id=1, source_target_pairs={{0,16},{4,20},{8,24},{12,28},{16,0},{20,4},{24,8},{28,12},{32,48},... | collective-permute-start | bytes 98312 | tf_op jit(solution)/shard_map/ppermute | solution.py:410
  94.3 2.3 %collective-permute-done.2 = f32[8,4,256]{2,1,0:T(4,128)S(1)} collective-permute-done((f32[8,4,256]{2,1,0:T(4,128)S(1)}, f32[8,4,256]{2,1,0:T(4,128)S(1)}, u32[]{:S(2)}, u32[]{:S(2)}) %collective-permute-start.2) | collective-permute-done | bytes 32800 | tf_op jit(solution)/shard_map/ppermute | solution.py:410
  96.6 0.9 collective-permute-start.3
  97.6 9.7 %collective-permute-done.3 = f32[4,4,256]{2,1,0:T(4,128)S(1)} collective-permute-done((f32[4,4,256]{2,1,0:T(4,128)S(1)}, f32[4,4,256]{2,1,0:T(4,128)S(1)}, u32[]{:S(2)}, u32[]{:S(2)}) %collective-permute-start.3) | collective-permute-done | bytes 16416 | tf_op jit(solution)/shard_map/ppermute | solution.py:410
  107.3 1.0 collective-permute-start.4
  108.3 3.0 %collective-permute-done.4 = f32[2,4,256]{2,1,0:T(4,128)S(1)} collective-permute-done((f32[2,4,256]{2,1,0:T(4,128)S(1)}, f32[2,4,256]{2,1,0:T(4,128)S(1)}, u32[]{:S(2)}, u32[]{:S(2)}) %collective-permute-start.4) | collective-permute-done | bytes 8224 | tf_op jit(solution)/shard_map/ppermute | solution.py:410
  111.3 5.6 %collective-permute-start.5 = (f32[1,4,256]{2,1,0:T(4,128)S(1)}, f32[1,4,256]{2,1,0:T(4,128)S(1)}, u32[]{:S(2)}, u32[]{:S(2)}) collective-permute-start(f32[1,4,256]{2,1,0:T(4,128)S(1)} %select_bitcast_fusion.5), channel_id=1, source_target_pairs={{0,128},{4,132},{8,136},{12,140},{16,144},{20,148},{24,152},{28,15... | collective-permute-start | bytes 12296 | tf_op jit(solution)/shard_map/ppermute | solution.py:410
  116.9 1.0 collective-permute-done.5
  117.9 0.0 all-to-all-done
  117.9 10.0 %add_rows.1 = f32[512,256]{1,0:T(8,128)} custom-call(f32[5376,128]{1,0:T(8,128)S(1)} %bitcast.114), custom_call_target="tpu_custom_call" | custom-call | tf_op jit(solution)/shard_map/add_rows/pallas_call | solution.py:384
  128.0 0.0 all-gather.2.cloned.1.call-update
  128.0 25.7 %all_to_all.15 = f32[64,4,256]{2,1,0:T(4,128)S(1)} all-to-all(f32[64,4,256]{2,1,0:T(4,128)S(1)} %broadcast_in_dim.17), channel_id=1, replica_groups=mesh['dom'=64,'rep'=4] {'dom'}, dimensions={0} | all-to-all | bytes 524288 | tf_op jit(solution)/shard_map/all_to_all | solution.py:462
  153.7 0.1 broadcast_in_dim.18
  153.8 0.1 broadcast_in_dim.19
  153.9 22.0 %all_to_all.16 = f32[4,256,256]{2,1,0:T(8,128)S(1)} all-to-all(f32[4,256,256]{2,1,0:T(8,128)S(1)} %broadcast_in_dim.19), channel_id=1, replica_groups=mesh['dom'=64,'rep'=4] {'rep'}, dimensions={0} | all-to-all | bytes 2097152 | tf_op jit(solution)/shard_map/all_to_all | solution.py:465
  175.9 0.0 all-gather.2.cloned.1.call-done.parts_ref
  175.9 0.0 copy-start
  175.9 1.6 copy-done
  177.5 1.9 %join_columns.1 = f32[2048,256]{1,0:T(8,128)} custom-call(f32[2048,256]{1,0:T(8,128)S(1)} %copy-done), custom_call_target="tpu_custom_call" | custom-call | tf_op jit(solution)/shard_map/join_columns/pallas_call | solution.py:395
  179.4 1.0 copy.121
  (13 shorter events, 0.2 us)
Async XLA Ops:
  31.8 86.2 %all-to-all-start = ((f32[256,1,2688]{2,1,0:T(1,128)}), f32[256,1,2688]{2,1,0:T(1,128)S(1)}, u32[]{:S(2)}, u32[]{:S(2)}) async-start(f32[256,1,2688]{2,1,0:T(1,128)} %bitcast.115), calls=%async_computation | async-start | bytes 5505024 | tf_op jit(solution)/shard_map/all_to_all | solution.py:455
  47.5 36.8 %reduce-scatter.2.cloned.1.call-start = ((), (), s32[]{:S(2)}) async-start(), calls=%async_computation.4 | async-start | bytes 1310720 | tf_op jit(solution)/shard_map/reduce_scatter | solution.py:458
  48.2 127.7 %all-gather.2.cloned.1.call-start = ((), (), s32[]{:S(2)}) async-start(), calls=%async_computation.5 | async-start | bytes 2621440 | tf_op jit(solution)/shard_map/all_gather | solution.py:469
  85.4 1.5 collective-permute-start
  86.9 4.9 %collective-permute-start.1 = (f32[16,4,256]{2,1,0:T(4,128)S(1)}, f32[16,4,256]{2,1,0:T(4,128)S(1)}, u32[]{:S(2)}, u32[]{:S(2)}) collective-permute-start(f32[16,4,256]{2,1,0:T(4,128)S(1)} %select_bitcast_fusion.1), channel_id=1, source_target_pairs={{0,8},{4,12},{8,0},{12,4},{16,24},{20,28},{24,16},{28,20},{32,40},... | collective-permute-start | bytes 196616 | tf_op jit(solution)/shard_map/ppermute | solution.py:410
  91.9 4.7 %collective-permute-start.2 = (f32[8,4,256]{2,1,0:T(4,128)S(1)}, f32[8,4,256]{2,1,0:T(4,128)S(1)}, u32[]{:S(2)}, u32[]{:S(2)}) collective-permute-start(f32[8,4,256]{2,1,0:T(4,128)S(1)} %select_bitcast_fusion.2), channel_id=1, source_target_pairs={{0,16},{4,20},{8,24},{12,28},{16,0},{20,4},{24,8},{28,12},{32,48},... | collective-permute-start | bytes 98312 | tf_op jit(solution)/shard_map/ppermute | solution.py:410
  96.6 10.6 %collective-permute-start.3 = (f32[4,4,256]{2,1,0:T(4,128)S(1)}, f32[4,4,256]{2,1,0:T(4,128)S(1)}, u32[]{:S(2)}, u32[]{:S(2)}) collective-permute-start(f32[4,4,256]{2,1,0:T(4,128)S(1)} %select_bitcast_fusion.3), channel_id=1, source_target_pairs={{0,32},{4,36},{8,40},{12,44},{16,48},{20,52},{24,56},{28,60},{32,0... | collective-permute-start | bytes 49160 | tf_op jit(solution)/shard_map/ppermute | solution.py:410
  107.3 4.0 %collective-permute-start.4 = (f32[2,4,256]{2,1,0:T(4,128)S(1)}, f32[2,4,256]{2,1,0:T(4,128)S(1)}, u32[]{:S(2)}, u32[]{:S(2)}) collective-permute-start(f32[2,4,256]{2,1,0:T(4,128)S(1)} %select_bitcast_fusion.4), channel_id=1, source_target_pairs={{0,64},{4,68},{8,72},{12,76},{16,80},{20,84},{24,88},{28,92},{32,9... | collective-permute-start | bytes 24584 | tf_op jit(solution)/shard_map/ppermute | solution.py:410
  111.3 6.6 %collective-permute-start.5 = (f32[1,4,256]{2,1,0:T(4,128)S(1)}, f32[1,4,256]{2,1,0:T(4,128)S(1)}, u32[]{:S(2)}, u32[]{:S(2)}) collective-permute-start(f32[1,4,256]{2,1,0:T(4,128)S(1)} %select_bitcast_fusion.5), channel_id=1, source_target_pairs={{0,128},{4,132},{8,136},{12,140},{16,144},{20,148},{24,152},{28,15... | collective-permute-start | bytes 12296 | tf_op jit(solution)/shard_map/ppermute | solution.py:410
  175.9 1.6 copy-start
Sparse Core Ops, SparseCore 0:
  51.4 32.8 reduce-scatter.1
  128.1 40.5 all-gather.1

commit v4 on v3

--- a/solution.py
+++ b/solution.py
@@ -264,67 +264,34 @@
 def add_kernel(capacity, lines_ref, table_ref):
     half = capacity // 2
     tall = half + 1
-    group = 64
-    chunk = group * tall
     sources = lines_ref.shape[0] // tall
     quarter = LANES // 2
     height = table_ref.shape[0]
-
-    def spot(shape, axis):
-        index = lax.broadcasted_iota(jnp.int32, shape, axis)
-        source = index // tall
-        return source, index - source * tall
-
-    def one(mask):
-        return mask.astype(F32).astype(BF16)
-
-    line_source, line_slot = spot((LANES, chunk), 1)
-    lane = lax.broadcasted_iota(jnp.int32, (LANES, chunk), 0)
-    real = line_slot < half
-    spread_first = one((lane == line_slot) & real)
-    spread_second = one((lane == line_slot + half) & real)
-    mine = line_source[:group, :] == lax.broadcasted_iota(jnp.int32, (group, chunk), 0)
-    col_source, _ = spot((chunk, group), 0)
-    expand = one(col_source == lax.broadcasted_iota(jnp.int32, (chunk, group), 1))
-    _, col_slot = spot((chunk, LANES), 0)
-    col_lane = lax.broadcasted_iota(jnp.int32, (chunk, LANES), 1)
-    col_real = col_slot < half
-    at_first = (col_lane == col_slot) & col_real
-    at_second = (col_lane == col_slot + half) & col_real
-    left = col_lane < quarter
-    place = lax.broadcasted_iota(jnp.int32, (height, chunk), 0)
+    codes = lines_ref[pl.ds(half, sources, stride=tall), :]
+    rows = codes.T.astype(jnp.int32) - 1
+    blocks = jnp.right_shift(codes.astype(jnp.int32) - 1, height.bit_length() - 1)
+    rows = jnp.where(rows < 0, -1, rows & (height - 1))
+    left = lax.broadcasted_iota(jnp.int32, (sources, LANES), 1) < quarter
+    sides = [jnp.where(left, 0, 1) + 2 * side for side in range(2)]
+    place = lax.broadcasted_iota(jnp.int32, (height, sources), 0)
     table_ref[...] = jnp.zeros(table_ref.shape, F32)
-
-    def step(c, _):
-        at = pl.multiple_of(c * chunk, 8)
-        codes = lines_ref[pl.ds(at + half, group, stride=tall), :]
-        lines = lines_ref[pl.ds(at, chunk), :]
-        swapped = pltpu.roll(lines, quarter, 1)
-        high = jnp.floor(codes * (1.0 / 16.0))
-        low = (codes - high * 16.0).astype(BF16)
-        high = high.astype(BF16)
-        grown = matmul(expand, high) * 16.0 + matmul(expand, low)
-        total = jnp.zeros(table_ref.shape, F32)
-        for spread, at_column, pair in (
-            (spread_first, at_first, jnp.where(left, lines, swapped)),
-            (spread_second, at_second, jnp.where(left, swapped, lines)),
-        ):
-            flat = matmul(high, spread) * 16.0 + matmul(low, spread)
-            row = jnp.sum(jnp.where(mine, flat, 0.0), axis=0, keepdims=True).astype(jnp.int32) - 1
-            column = jnp.sum(jnp.where(at_column, grown, 0.0), axis=1, keepdims=True)
-            column = column.astype(jnp.int32) - 1
-            block = jnp.where(column < 0, -1, jnp.right_shift(column, 9))
-            kept = [
-                jnp.where(block == 2 * side + jnp.where(left, 0, 1), pair, 0.0).astype(BF16)
-                for side in range(2)
-            ]
-            wide = jnp.concatenate(kept, axis=1)
-            picker = one((row & (height - 1)) == place)
-            total = total + matmul(picker, wide)
-        table_ref[...] += total
-        return 0
-
-    lax.fori_loop(0, sources // group, step, 0)
+    together = 5
+    for start in range(0, half, together):
+        pickers, wides = [], []
+        for slot in range(start, min(start + together, half)):
+            lines = lines_ref[pl.ds(slot, sources, stride=tall), :]
+            swapped = pltpu.roll(lines, quarter, 1)
+            for at, pair in (
+                (slot, jnp.where(left, lines, swapped)),
+                (slot + half, jnp.where(left, swapped, lines)),
+            ):
+                block = blocks[:, at : at + 1]
+                kept = [jnp.where(block == side, pair, 0.0).astype(BF16) for side in sides]
+                wides.append(jnp.concatenate(kept, axis=1))
+                pickers.append((rows[at : at + 1, :] == place).astype(F32).astype(BF16))
+        table_ref[...] += matmul(
+            jnp.concatenate(pickers, axis=1), jnp.concatenate(wides, axis=0)
+        )
 
 
 def join_kernel(parts_ref, table_ref):
@@ -462,8 +429,24 @@
     whole = lax.all_to_all(
         jnp.broadcast_to(total[None], (domains, share, width)), "dom", 0, 0, tiled=True
     ).reshape(width, width)
-    weight_grads = lax.all_to_all(
-        jnp.broadcast_to(whole[None], (REPS, width, width)), "rep", 0, 0, tiled=True
+    place = lax.axis_index("rep")
+    parts = [whole] + [
+        lax.ppermute(whole, "rep", [(i, (i + step) % REPS) for i in range(REPS)])
+        for step in range(1, REPS)
+    ]
+    weight_grads = jnp.stack(
+        [
+            jnp.where(
+                place == matrix,
+                parts[0],
+                jnp.where(
+                    place == (matrix + 1) % REPS,
+                    parts[1],
+                    jnp.where(place == (matrix + 2) % REPS, parts[2], parts[3]),
+                ),
+            )
+            for matrix in range(REPS)
+        ]
     )
     quarter = add_rows(capacity, arrived.reshape(-1, LANES))
     table = join_columns(lax.all_gather(quarter, "rep", axis=0, tiled=True))

time: 188 us -> 183 us (0.973)
  blocking collectives: 47.7 us -> 25.7 us
  waiting for transfers between devices: 57.9 us -> 75.2 us
  Pallas kernels: 36.5 us -> 31.2 us
  starting transfers between devices: 26.9 us -> 31.8 us
    all_to_all x1 -> x0, blocking collectives: 22 us -> none  [on_device(): lax.all_to_all(jnp.broadcast_to(whole[None], (REPS, width, width)), 'rep'...]
    ppermute x0 -> x3, waiting for transfers between devices: none -> 17.3 us  [on_device(): lax.ppermute(whole, 'rep', [(i, (i + step) % REPS) for i in range(REPS)])]
    pallas_call x1, Pallas kernels: 10 us -> 4.71 us  [add_rows(): pl.pallas_call(functools.partial(add_kernel, capacity), out_shape=jax.Sha...]
    ppermute x0 -> x3, starting transfers between devices: none -> 4.87 us  [on_device(): lax.ppermute(whole, 'rep', [(i, (i + step) % REPS) for i in range(REPS)])]
  transfers between devices with their start and end apart: 9 -> 12, of which waited for: 7 -> 9; matrix products, arithmetic and copies ran while one was open for 1% -> 1% of each run, Pallas kernels for 0% -> 0%
where the time goes in v4:
time: 183 us; the launch traced here: 182 us
  waiting for transfers between devices  75.2 us (41%)
  starting transfers between devices  31.8 us (17%)
  Pallas kernels  31.2 us (17%)
  blocking collectives  25.7 us (14%)
  between operations  14.2 us (8%)
  local copies, waits for them, and re-layouts  2.74 us (1%)
    reduce_scatter x1, waiting for transfers between devices, on_device(): own_grads = lax.psum_scatter(grads, 'rep', scatter_dimension=0, tiled=True)  36.1 us
    all_to_all x1, blocking collectives, on_device(): lax.all_to_all(jnp.broadcast_to(total[None], (domains, share, width)), 'd...  25.7 us
    pallas_call x1, Pallas kernels, local_pass(): pl.pallas_call(functools.partial(local_kernel, capacity), out_shape=(jax....  24.6 us
    ppermute x6, waiting for transfers between devices, swap(): return lax.ppermute(part, 'dom', [(i, i ^ step) for i in range(domains)])  21.1 us
    ppermute x3, waiting for transfers between devices, on_device(): lax.ppermute(whole, 'rep', [(i, (i + step) % REPS) for i in range(REPS)])  17.3 us
    all_to_all x1, starting transfers between devices, on_device(): lax.all_to_all(outgoing.reshape(REPS * domains, 1, -1), ('rep', 'dom'), 0...  15.7 us
    ppermute x6, starting transfers between devices, swap(): return lax.ppermute(part, 'dom', [(i, i ^ step) for i in range(domains)])  11.2 us
    ppermute x3, starting transfers between devices, on_device(): lax.ppermute(whole, 'rep', [(i, (i + step) % REPS) for i in range(REPS)])  4.87 us
  transfers between devices with their start and end apart: 12, of which 9 were waited for; matrix products, arithmetic and copies ran while one was open for 1% of the time, Pallas kernels for 0%

profile of v4, /device:TPU:1, one launch (start us, length us, event | category | flops | bytes accessed | tf_op | source)
XLA Modules:
  0.0 182.2 jit_solution(13277537686342309577)
XLA Ops:
  7.2 24.6 %local_pass.1 = (f32[5376,128]{1,0:T(8,128)}, f32[1024,256]{1,0:T(8,128)}) custom-call(bf16[4096,256]{1,0:T(8,128)(2,1)} %x_hbm.1, s32[15,1024]{1,0:T(8,128)} %bitcast.132, s32[10,128]{1,0:T(8,128)} %bitcast.133, s32[1,4096]{1,0:T(1,128)} %ids_hbm.1, s32[1,2048]{1,0:T(1,128)} %bitcast.134, s32[1,2048]{1,0:T(1,128)} %bitcast.135, bf16[128,256]{1,0:T(8,128)(2,1)} %cot_hbm.1, ...), custom_call_target="tpu_custom_call" | custom-call | tf_op jit(solution)/shard_map/local_pass/pallas_call | solution.py:321
  31.8 15.7 %all-to-all-start = ((f32[256,1,2688]{2,1,0:T(1,128)}), f32[256,1,2688]{2,1,0:T(1,128)S(1)}, u32[]{:S(2)}, u32[]{:S(2)}) async-start(f32[256,1,2688]{2,1,0:T(1,128)} %bitcast.123), calls=%async_computation | async-start | bytes 5505024 | tf_op jit(solution)/shard_map/all_to_all | solution.py:422
  47.5 0.0 reduce-scatter.2.cloned.1.call-start
  47.5 0.7 reduce-scatter.2.cloned.1.call-update
  48.2 0.0 all-gather.2.cloned.1.call-start
  48.2 36.1 %reduce-scatter.2.cloned.1.call-done = f32[256,256]{1,0:T(8,128)} async-done(((f32[1024,256]{1,0:T(8,128)}), f32[256,256]{1,0:T(8,128)}) %reduce-scatter.2.cloned.1.call-update) | async-done | bytes 262160 | tf_op jit(solution)/shard_map/reduce_scatter | solution.py:425
  84.3 1.0 reshape_reshape.3
  85.4 0.5 collective-permute-start
  85.9 1.0 collective-permute-done
  86.9 0.8 collective-permute-start.1
  87.7 4.1 %collective-permute-done.1 = f32[16,4,256]{2,1,0:T(4,128)S(1)} collective-permute-done((f32[16,4,256]{2,1,0:T(4,128)S(1)}, f32[16,4,256]{2,1,0:T(4,128)S(1)}, u32[]{:S(2)}, u32[]{:S(2)}) %collective-permute-start.1) | collective-permute-done | bytes 65568 | tf_op jit(solution)/shard_map/ppermute | solution.py:377
  91.9 2.4 %collective-permute-start.2 = (f32[8,4,256]{2,1,0:T(4,128)S(1)}, f32[8,4,256]{2,1,0:T(4,128)S(1)}, u32[]{:S(2)}, u32[]{:S(2)}) collective-permute-start(f32[8,4,256]{2,1,0:T(4,128)S(1)} %select_bitcast_fusion.6), channel_id=1, source_target_pairs={{0,16},{4,20},{8,24},{12,28},{16,0},{20,4},{24,8},{28,12},{32,48},... | collective-permute-start | bytes 98312 | tf_op jit(solution)/shard_map/ppermute | solution.py:377
  94.3 2.3 %collective-permute-done.2 = f32[8,4,256]{2,1,0:T(4,128)S(1)} collective-permute-done((f32[8,4,256]{2,1,0:T(4,128)S(1)}, f32[8,4,256]{2,1,0:T(4,128)S(1)}, u32[]{:S(2)}, u32[]{:S(2)}) %collective-permute-start.2) | collective-permute-done | bytes 32800 | tf_op jit(solution)/shard_map/ppermute | solution.py:377
  96.6 0.9 collective-permute-start.3
  97.6 9.7 %collective-permute-done.3 = f32[4,4,256]{2,1,0:T(4,128)S(1)} collective-permute-done((f32[4,4,256]{2,1,0:T(4,128)S(1)}, f32[4,4,256]{2,1,0:T(4,128)S(1)}, u32[]{:S(2)}, u32[]{:S(2)}) %collective-permute-start.3) | collective-permute-done | bytes 16416 | tf_op jit(solution)/shard_map/ppermute | solution.py:377
  107.3 1.0 collective-permute-start.4
  108.3 3.0 %collective-permute-done.4 = f32[2,4,256]{2,1,0:T(4,128)S(1)} collective-permute-done((f32[2,4,256]{2,1,0:T(4,128)S(1)}, f32[2,4,256]{2,1,0:T(4,128)S(1)}, u32[]{:S(2)}, u32[]{:S(2)}) %collective-permute-start.4) | collective-permute-done | bytes 8224 | tf_op jit(solution)/shard_map/ppermute | solution.py:377
  111.3 5.6 %collective-permute-start.5 = (f32[1,4,256]{2,1,0:T(4,128)S(1)}, f32[1,4,256]{2,1,0:T(4,128)S(1)}, u32[]{:S(2)}, u32[]{:S(2)}) collective-permute-start(f32[1,4,256]{2,1,0:T(4,128)S(1)} %select_bitcast_fusion.9), channel_id=1, source_target_pairs={{0,128},{4,132},{8,136},{12,140},{16,144},{20,148},{24,152},{28,15... | collective-permute-start | bytes 12296 | tf_op jit(solution)/shard_map/ppermute | solution.py:377
  116.9 1.0 collective-permute-done.5
  117.9 4.7 %add_rows.1 = f32[512,256]{1,0:T(8,128)} custom-call(f32[5376,128]{1,0:T(8,128)S(1)} %bitcast.122), custom_call_target="tpu_custom_call" | custom-call | tf_op jit(solution)/shard_map/add_rows/pallas_call | solution.py:351
  122.6 0.0 all-gather.2.cloned.1.call-update
  122.7 25.7 %all_to_all.10 = f32[64,4,256]{2,1,0:T(4,128)S(1)} all-to-all(f32[64,4,256]{2,1,0:T(4,128)S(1)} %broadcast_in_dim.10), channel_id=1, replica_groups=mesh['dom'=64,'rep'=4] {'dom'}, dimensions={0} | all-to-all | bytes 524288 | tf_op jit(solution)/shard_map/all_to_all | solution.py:429
  148.4 0.1 reshape.102
  148.5 1.3 collective-permute-start.6
  149.8 2.4 %collective-permute-start.7 = (f32[256,256]{1,0:T(8,128)S(1)}, f32[256,256]{1,0:T(8,128)S(1)}, u32[]{:S(2)}, u32[]{:S(2)}) collective-permute-start(f32[256,256]{1,0:T(8,128)S(1)} %reshape.102), channel_id=1, source_target_pairs={{0,2},{1,3},{2,0},{3,1},{4,6},{5,7},{6,4},{7,5},{8,10},{9,11},{10,... | collective-permute-start | bytes 786440 | tf_op jit(solution)/shard_map/ppermute | solution.py:434
  152.2 1.2 collective-permute-start.8
  153.4 10.2 %collective-permute-done.6 = f32[256,256]{1,0:T(8,128)S(1)} collective-permute-done((f32[256,256]{1,0:T(8,128)S(1)}, f32[256,256]{1,0:T(8,128)S(1)}, u32[]{:S(2)}, u32[]{:S(2)}) %collective-permute-start.6) | collective-permute-done | bytes 262176 | tf_op jit(solution)/shard_map/ppermute | solution.py:434
  163.6 7.1 %collective-permute-done.7 = f32[256,256]{1,0:T(8,128)S(1)} collective-permute-done((f32[256,256]{1,0:T(8,128)S(1)}, f32[256,256]{1,0:T(8,128)S(1)}, u32[]{:S(2)}, u32[]{:S(2)}) %collective-permute-start.7) | collective-permute-done | bytes 262176 | tf_op jit(solution)/shard_map/ppermute | solution.py:434
  170.7 0.1 select_bitcast_fusion.3
  170.8 1.0 pad_maximum_fusion
  171.9 1.6 copy-done
  173.5 1.9 %join_columns.1 = f32[2048,256]{1,0:T(8,128)} custom-call(f32[2048,256]{1,0:T(8,128)S(1)} %copy-done), custom_call_target="tpu_custom_call" | custom-call | tf_op jit(solution)/shard_map/join_columns/pallas_call | solution.py:362
  (17 shorter events, 0.2 us)
Async XLA Ops:
  31.8 86.2 %all-to-all-start = ((f32[256,1,2688]{2,1,0:T(1,128)}), f32[256,1,2688]{2,1,0:T(1,128)S(1)}, u32[]{:S(2)}, u32[]{:S(2)}) async-start(f32[256,1,2688]{2,1,0:T(1,128)} %bitcast.123), calls=%async_computation | async-start | bytes 5505024 | tf_op jit(solution)/shard_map/all_to_all | solution.py:422
  47.5 36.8 %reduce-scatter.2.cloned.1.call-start = ((), (), s32[]{:S(2)}) async-start(), calls=%async_computation.3 | async-start | bytes 1310720 | tf_op jit(solution)/shard_map/reduce_scatter | solution.py:425
  48.2 123.7 %all-gather.2.cloned.1.call-start = ((), (), s32[]{:S(2)}) async-start(), calls=%async_computation.4 | async-start | bytes 2621440 | tf_op jit(solution)/shard_map/all_gather | solution.py:452
  85.4 1.5 collective-permute-start
  86.9 4.9 %collective-permute-start.1 = (f32[16,4,256]{2,1,0:T(4,128)S(1)}, f32[16,4,256]{2,1,0:T(4,128)S(1)}, u32[]{:S(2)}, u32[]{:S(2)}) collective-permute-start(f32[16,4,256]{2,1,0:T(4,128)S(1)} %select_bitcast_fusion.5), channel_id=1, source_target_pairs={{0,8},{4,12},{8,0},{12,4},{16,24},{20,28},{24,16},{28,20},{32,40},... | collective-permute-start | bytes 196616 | tf_op jit(solution)/shard_map/ppermute | solution.py:377
  91.9 4.7 %collective-permute-start.2 = (f32[8,4,256]{2,1,0:T(4,128)S(1)}, f32[8,4,256]{2,1,0:T(4,128)S(1)}, u32[]{:S(2)}, u32[]{:S(2)}) collective-permute-start(f32[8,4,256]{2,1,0:T(4,128)S(1)} %select_bitcast_fusion.6), channel_id=1, source_target_pairs={{0,16},{4,20},{8,24},{12,28},{16,0},{20,4},{24,8},{28,12},{32,48},... | collective-permute-start | bytes 98312 | tf_op jit(solution)/shard_map/ppermute | solution.py:377
  96.6 10.6 %collective-permute-start.3 = (f32[4,4,256]{2,1,0:T(4,128)S(1)}, f32[4,4,256]{2,1,0:T(4,128)S(1)}, u32[]{:S(2)}, u32[]{:S(2)}) collective-permute-start(f32[4,4,256]{2,1,0:T(4,128)S(1)} %select_bitcast_fusion.7), channel_id=1, source_target_pairs={{0,32},{4,36},{8,40},{12,44},{16,48},{20,52},{24,56},{28,60},{32,0... | collective-permute-start | bytes 49160 | tf_op jit(solution)/shard_map/ppermute | solution.py:377
  107.3 4.0 %collective-permute-start.4 = (f32[2,4,256]{2,1,0:T(4,128)S(1)}, f32[2,4,256]{2,1,0:T(4,128)S(1)}, u32[]{:S(2)}, u32[]{:S(2)}) collective-permute-start(f32[2,4,256]{2,1,0:T(4,128)S(1)} %select_bitcast_fusion.8), channel_id=1, source_target_pairs={{0,64},{4,68},{8,72},{12,76},{16,80},{20,84},{24,88},{28,92},{32,9... | collective-permute-start | bytes 24584 | tf_op jit(solution)/shard_map/ppermute | solution.py:377
  111.3 6.6 %collective-permute-start.5 = (f32[1,4,256]{2,1,0:T(4,128)S(1)}, f32[1,4,256]{2,1,0:T(4,128)S(1)}, u32[]{:S(2)}, u32[]{:S(2)}) collective-permute-start(f32[1,4,256]{2,1,0:T(4,128)S(1)} %select_bitcast_fusion.9), channel_id=1, source_target_pairs={{0,128},{4,132},{8,136},{12,140},{16,144},{20,148},{24,152},{28,15... | collective-permute-start | bytes 12296 | tf_op jit(solution)/shard_map/ppermute | solution.py:377
  148.5 15.1 %collective-permute-start.6 = (f32[256,256]{1,0:T(8,128)S(1)}, f32[256,256]{1,0:T(8,128)S(1)}, u32[]{:S(2)}, u32[]{:S(2)}) collective-permute-start(f32[256,256]{1,0:T(8,128)S(1)} %reshape.102), channel_id=1, source_target_pairs={{0,1},{1,2},{2,3},{3,0},{4,5},{5,6},{6,7},{7,4},{8,9},{9,10},{10,1... | collective-permute-start | bytes 786440 | tf_op jit(solution)/shard_map/ppermute | solution.py:434
  149.8 20.9 %collective-permute-start.7 = (f32[256,256]{1,0:T(8,128)S(1)}, f32[256,256]{1,0:T(8,128)S(1)}, u32[]{:S(2)}, u32[]{:S(2)}) collective-permute-start(f32[256,256]{1,0:T(8,128)S(1)} %reshape.102), channel_id=1, source_target_pairs={{0,2},{1,3},{2,0},{3,1},{4,6},{5,7},{6,4},{7,5},{8,10},{9,11},{10,... | collective-permute-start | bytes 786440 | tf_op jit(solution)/shard_map/ppermute | solution.py:434
  152.2 18.5 %collective-permute-start.8 = (f32[256,256]{1,0:T(8,128)S(1)}, f32[256,256]{1,0:T(8,128)S(1)}, u32[]{:S(2)}, u32[]{:S(2)}) collective-permute-start(f32[256,256]{1,0:T(8,128)S(1)} %reshape.102), channel_id=1, source_target_pairs={{0,3},{1,0},{2,1},{3,2},{4,7},{5,4},{6,5},{7,6},{8,11},{9,8},{10,9... | collective-permute-start | bytes 786440 | tf_op jit(solution)/shard_map/ppermute | solution.py:434
  171.9 1.6 copy-start
Sparse Core Ops, SparseCore 0:
  51.4 32.8 reduce-scatter.1
  122.8 42.4 all-gather.1

commit v5 on v4

--- a/solution.py
+++ b/solution.py
@@ -426,15 +426,12 @@
     share = width // domains
     total = sum_over_domains(own_grads.reshape(domains, share, width), domains) * factor
     arrived, total = lax.optimization_barrier((arrived, total))
-    whole = lax.all_to_all(
-        jnp.broadcast_to(total[None], (domains, share, width)), "dom", 0, 0, tiled=True
-    ).reshape(width, width)
     place = lax.axis_index("rep")
-    parts = [whole] + [
-        lax.ppermute(whole, "rep", [(i, (i + step) % REPS) for i in range(REPS)])
+    parts = [total] + [
+        lax.ppermute(total, "rep", [(i, (i + step) % REPS) for i in range(REPS)])
         for step in range(1, REPS)
     ]
-    weight_grads = jnp.stack(
+    totals = jnp.concatenate(
         [
             jnp.where(
                 place == matrix,
@@ -446,7 +443,16 @@
                 ),
             )
             for matrix in range(REPS)
-        ]
+        ],
+        axis=0,
+    )
+    spread = lax.all_to_all(
+        jnp.broadcast_to(totals[None], (domains, REPS * share, width)), "dom", 0, 0, tiled=True
+    )
+    weight_grads = (
+        spread.reshape(domains, REPS, share, width)
+        .transpose(1, 0, 2, 3)
+        .reshape(REPS, width, width)
     )
     quarter = add_rows(capacity, arrived.reshape(-1, LANES))
     table = join_columns(lax.all_gather(quarter, "rep", axis=0, tiled=True))

time: 183 us -> 184 us (level)
  blocking collectives: 25.7 us -> 42.2 us
  waiting for transfers between devices: 75.2 us -> 59.2 us
  local copies, waits for them, and re-layouts: 2.74 us -> 5.18 us
    all_to_all x1, blocking collectives: 25.7 us -> 42.2 us  [on_device(): lax.all_to_all(jnp.broadcast_to(totals[None], (domains, REPS * share, wid...]
    ppermute x3, waiting for transfers between devices: 17.3 us -> 1.29 us  [on_device(): lax.ppermute(total, 'rep', [(i, (i + step) % REPS) for i in range(REPS)])]
  transfers between devices with their start and end apart: 12 -> 12, of which waited for: 9 -> 9; matrix products, arithmetic and copies ran while one was open for 1% -> 2% of each run, Pallas kernels for 0% -> 0%
where the time goes in v5:
time: 184 us
  waiting for transfers between devices  59.2 us (32%)
  blocking collectives  42.2 us (23%)
  starting transfers between devices  31.9 us (17%)
  Pallas kernels  31.2 us (17%)
  between operations  14.2 us (8%)
  local copies, waits for them, and re-layouts  5.18 us (3%)
    all_to_all x1, blocking collectives, on_device(): lax.all_to_all(jnp.broadcast_to(totals[None], (domains, REPS * share, wid...  42.2 us
    reduce_scatter x1, waiting for transfers between devices, on_device(): own_grads = lax.psum_scatter(grads, 'rep', scatter_dimension=0, tiled=True)  36.1 us
    pallas_call x1, Pallas kernels, local_pass(): pl.pallas_call(functools.partial(local_kernel, capacity), out_shape=(jax....  24.6 us
    ppermute x6, waiting for transfers between devices, swap(): return lax.ppermute(part, 'dom', [(i, i ^ step) for i in range(domains)])  21.1 us
    all_to_all x1, starting transfers between devices, on_device(): lax.all_to_all(outgoing.reshape(REPS * domains, 1, -1), ('rep', 'dom'), 0...  15.7 us
    ppermute x6, starting transfers between devices, swap(): return lax.ppermute(part, 'dom', [(i, i ^ step) for i in range(domains)])  11.2 us
    ppermute x3, starting transfers between devices, on_device(): lax.ppermute(total, 'rep', [(i, (i + step) % REPS) for i in range(REPS)])  4.9 us
    pallas_call x1, Pallas kernels, add_rows(): pl.pallas_call(functools.partial(add_kernel, capacity), out_shape=jax.Sha...  4.71 us
  transfers between devices with their start and end apart: 12, of which 9 were waited for; matrix products, arithmetic and copies ran while one was open for 2% of the time, Pallas kernels for 0%

profile of v5, /device:TPU:1, one launch (start us, length us, event | category | flops | bytes accessed | tf_op | source)
XLA Modules:
  0.0 184.0 jit_solution(10745354767456581877)
XLA Ops:
  7.2 24.6 %local_pass.1 = (f32[5376,128]{1,0:T(8,128)}, f32[1024,256]{1,0:T(8,128)}) custom-call(bf16[4096,256]{1,0:T(8,128)(2,1)} %x_hbm.1, s32[15,1024]{1,0:T(8,128)} %bitcast.130, s32[10,128]{1,0:T(8,128)} %bitcast.131, s32[1,4096]{1,0:T(1,128)} %ids_hbm.1, s32[1,2048]{1,0:T(1,128)} %bitcast.132, s32[1,2048]{1,0:T(1,128)} %bitcast.133, bf16[128,256]{1,0:T(8,128)(2,1)} %cot_hbm.1, ...), custom_call_target="tpu_custom_call" | custom-call | tf_op jit(solution)/shard_map/local_pass/pallas_call | solution.py:321
  31.8 15.7 %all-to-all-start = ((f32[256,1,2688]{2,1,0:T(1,128)}), f32[256,1,2688]{2,1,0:T(1,128)S(1)}, u32[]{:S(2)}, u32[]{:S(2)}) async-start(f32[256,1,2688]{2,1,0:T(1,128)} %bitcast.121), calls=%async_computation | async-start | bytes 5505024 | tf_op jit(solution)/shard_map/all_to_all | solution.py:422
  47.5 0.0 reduce-scatter.2.cloned.1.call-start
  47.5 0.7 reduce-scatter.2.cloned.1.call-update
  48.2 0.0 all-gather.2.cloned.1.call-start
  48.2 36.1 %reduce-scatter.2.cloned.1.call-done = f32[256,256]{1,0:T(8,128)} async-done(((f32[1024,256]{1,0:T(8,128)}), f32[256,256]{1,0:T(8,128)}) %reduce-scatter.2.cloned.1.call-update) | async-done | bytes 262160 | tf_op jit(solution)/shard_map/reduce_scatter | solution.py:425
  84.3 1.0 reshape_reshape.3
  85.4 0.5 collective-permute-start
  85.9 1.0 collective-permute-done
  86.9 0.8 collective-permute-start.1
  87.7 4.1 %collective-permute-done.1 = f32[16,4,256]{2,1,0:T(4,128)S(1)} collective-permute-done((f32[16,4,256]{2,1,0:T(4,128)S(1)}, f32[16,4,256]{2,1,0:T(4,128)S(1)}, u32[]{:S(2)}, u32[]{:S(2)}) %collective-permute-start.1) | collective-permute-done | bytes 65568 | tf_op jit(solution)/shard_map/ppermute | solution.py:377
  91.9 2.4 %collective-permute-start.2 = (f32[8,4,256]{2,1,0:T(4,128)S(1)}, f32[8,4,256]{2,1,0:T(4,128)S(1)}, u32[]{:S(2)}, u32[]{:S(2)}) collective-permute-start(f32[8,4,256]{2,1,0:T(4,128)S(1)} %select_bitcast_fusion.2), channel_id=1, source_target_pairs={{0,16},{4,20},{8,24},{12,28},{16,0},{20,4},{24,8},{28,12},{32,48},... | collective-permute-start | bytes 98312 | tf_op jit(solution)/shard_map/ppermute | solution.py:377
  94.3 2.3 %collective-permute-done.2 = f32[8,4,256]{2,1,0:T(4,128)S(1)} collective-permute-done((f32[8,4,256]{2,1,0:T(4,128)S(1)}, f32[8,4,256]{2,1,0:T(4,128)S(1)}, u32[]{:S(2)}, u32[]{:S(2)}) %collective-permute-start.2) | collective-permute-done | bytes 32800 | tf_op jit(solution)/shard_map/ppermute | solution.py:377
  96.6 0.9 collective-permute-start.3
  97.6 9.7 %collective-permute-done.3 = f32[4,4,256]{2,1,0:T(4,128)S(1)} collective-permute-done((f32[4,4,256]{2,1,0:T(4,128)S(1)}, f32[4,4,256]{2,1,0:T(4,128)S(1)}, u32[]{:S(2)}, u32[]{:S(2)}) %collective-permute-start.3) | collective-permute-done | bytes 16416 | tf_op jit(solution)/shard_map/ppermute | solution.py:377
  107.3 1.0 collective-permute-start.4
  108.3 3.0 %collective-permute-done.4 = f32[2,4,256]{2,1,0:T(4,128)S(1)} collective-permute-done((f32[2,4,256]{2,1,0:T(4,128)S(1)}, f32[2,4,256]{2,1,0:T(4,128)S(1)}, u32[]{:S(2)}, u32[]{:S(2)}) %collective-permute-start.4) | collective-permute-done | bytes 8224 | tf_op jit(solution)/shard_map/ppermute | solution.py:377
  111.3 5.6 %collective-permute-start.5 = (f32[1,4,256]{2,1,0:T(4,128)S(1)}, f32[1,4,256]{2,1,0:T(4,128)S(1)}, u32[]{:S(2)}, u32[]{:S(2)}) collective-permute-start(f32[1,4,256]{2,1,0:T(4,128)S(1)} %select_bitcast_fusion.5), channel_id=1, source_target_pairs={{0,128},{4,132},{8,136},{12,140},{16,144},{20,148},{24,152},{28,15... | collective-permute-start | bytes 12296 | tf_op jit(solution)/shard_map/ppermute | solution.py:377
  116.9 1.0 collective-permute-done.5
  117.9 4.7 %add_rows.1 = f32[512,256]{1,0:T(8,128)} custom-call(f32[5376,128]{1,0:T(8,128)S(1)} %bitcast.118), custom_call_target="tpu_custom_call" | custom-call | tf_op jit(solution)/shard_map/add_rows/pallas_call | solution.py:351
  122.7 1.3 collective-permute-start.6
  124.0 2.4 %collective-permute-start.7 = (f32[4,256]{1,0:T(4,128)S(1)}, f32[4,256]{1,0:T(4,128)S(1)}, u32[]{:S(2)}, u32[]{:S(2)}) collective-permute-start(f32[4,256]{1,0:T(4,128)S(1)} %fusion.10), channel_id=1, source_target_pairs={{0,2},{1,3},{2,0},{3,1},{4,6},{5,7},{6,4},{7,5},{8,10},{9,11},{10,... | collective-permute-start | bytes 12296 | tf_op jit(solution)/shard_map/ppermute | solution.py:431
  126.4 1.2 collective-permute-start.8
  127.6 0.4 collective-permute-done.7
  128.0 0.9 collective-permute-done.8
  128.9 0.1 broadcast_in_dim.10
  129.0 42.2 %all_to_all.10 = f32[64,16,256]{2,1,0:T(8,128)S(1)} all-to-all(f32[64,16,256]{2,1,0:T(8,128)S(1)} %broadcast_in_dim.10), channel_id=1, replica_groups=mesh['dom'=64,'rep'=4] {'dom'}, dimensions={0} | all-to-all | bytes 2097152 | tf_op jit(solution)/shard_map/all_to_all | solution.py:449
  171.2 0.6 copy.142
  171.8 0.7 copy.143
  172.5 1.2 copy.144
  173.7 1.6 copy-done
  175.2 1.9 %join_columns.1 = f32[2048,256]{1,0:T(8,128)} custom-call(f32[2048,256]{1,0:T(8,128)S(1)} %copy-done), custom_call_target="tpu_custom_call" | custom-call | tf_op jit(solution)/shard_map/join_columns/pallas_call | solution.py:362
  (19 shorter events, 0.2 us)
Async XLA Ops:
  31.8 86.2 %all-to-all-start = ((f32[256,1,2688]{2,1,0:T(1,128)}), f32[256,1,2688]{2,1,0:T(1,128)S(1)}, u32[]{:S(2)}, u32[]{:S(2)}) async-start(f32[256,1,2688]{2,1,0:T(1,128)} %bitcast.121), calls=%async_computation | async-start | bytes 5505024 | tf_op jit(solution)/shard_map/all_to_all | solution.py:422
  47.5 36.8 %reduce-scatter.2.cloned.1.call-start = ((), (), s32[]{:S(2)}) async-start(), calls=%async_computation.3 | async-start | bytes 1310720 | tf_op jit(solution)/shard_map/reduce_scatter | solution.py:425
  48.2 125.5 %all-gather.2.cloned.1.call-start = ((), (), s32[]{:S(2)}) async-start(), calls=%async_computation.4 | async-start | bytes 2621440 | tf_op jit(solution)/shard_map/all_gather | solution.py:458
  85.4 1.5 collective-permute-start
  86.9 4.9 %collective-permute-start.1 = (f32[16,4,256]{2,1,0:T(4,128)S(1)}, f32[16,4,256]{2,1,0:T(4,128)S(1)}, u32[]{:S(2)}, u32[]{:S(2)}) collective-permute-start(f32[16,4,256]{2,1,0:T(4,128)S(1)} %select_bitcast_fusion.1), channel_id=1, source_target_pairs={{0,8},{4,12},{8,0},{12,4},{16,24},{20,28},{24,16},{28,20},{32,40},... | collective-permute-start | bytes 196616 | tf_op jit(solution)/shard_map/ppermute | solution.py:377
  91.9 4.7 %collective-permute-start.2 = (f32[8,4,256]{2,1,0:T(4,128)S(1)}, f32[8,4,256]{2,1,0:T(4,128)S(1)}, u32[]{:S(2)}, u32[]{:S(2)}) collective-permute-start(f32[8,4,256]{2,1,0:T(4,128)S(1)} %select_bitcast_fusion.2), channel_id=1, source_target_pairs={{0,16},{4,20},{8,24},{12,28},{16,0},{20,4},{24,8},{28,12},{32,48},... | collective-permute-start | bytes 98312 | tf_op jit(solution)/shard_map/ppermute | solution.py:377
  96.6 10.6 %collective-permute-start.3 = (f32[4,4,256]{2,1,0:T(4,128)S(1)}, f32[4,4,256]{2,1,0:T(4,128)S(1)}, u32[]{:S(2)}, u32[]{:S(2)}) collective-permute-start(f32[4,4,256]{2,1,0:T(4,128)S(1)} %select_bitcast_fusion.3), channel_id=1, source_target_pairs={{0,32},{4,36},{8,40},{12,44},{16,48},{20,52},{24,56},{28,60},{32,0... | collective-permute-start | bytes 49160 | tf_op jit(solution)/shard_map/ppermute | solution.py:377
  107.3 4.0 %collective-permute-start.4 = (f32[2,4,256]{2,1,0:T(4,128)S(1)}, f32[2,4,256]{2,1,0:T(4,128)S(1)}, u32[]{:S(2)}, u32[]{:S(2)}) collective-permute-start(f32[2,4,256]{2,1,0:T(4,128)S(1)} %select_bitcast_fusion.4), channel_id=1, source_target_pairs={{0,64},{4,68},{8,72},{12,76},{16,80},{20,84},{24,88},{28,92},{32,9... | collective-permute-start | bytes 24584 | tf_op jit(solution)/shard_map/ppermute | solution.py:377
  111.3 6.6 %collective-permute-start.5 = (f32[1,4,256]{2,1,0:T(4,128)S(1)}, f32[1,4,256]{2,1,0:T(4,128)S(1)}, u32[]{:S(2)}, u32[]{:S(2)}) collective-permute-start(f32[1,4,256]{2,1,0:T(4,128)S(1)} %select_bitcast_fusion.5), channel_id=1, source_target_pairs={{0,128},{4,132},{8,136},{12,140},{16,144},{20,148},{24,152},{28,15... | collective-permute-start | bytes 12296 | tf_op jit(solution)/shard_map/ppermute | solution.py:377
  122.7 4.9 %collective-permute-start.6 = (f32[4,256]{1,0:T(4,128)S(1)}, f32[4,256]{1,0:T(4,128)S(1)}, u32[]{:S(2)}, u32[]{:S(2)}) collective-permute-start(f32[4,256]{1,0:T(4,128)S(1)} %fusion.10), channel_id=1, source_target_pairs={{0,1},{1,2},{2,3},{3,0},{4,5},{5,6},{6,7},{7,4},{8,9},{9,10},{10,1... | collective-permute-start | bytes 12296 | tf_op jit(solution)/shard_map/ppermute | solution.py:431
  124.0 4.0 %collective-permute-start.7 = (f32[4,256]{1,0:T(4,128)S(1)}, f32[4,256]{1,0:T(4,128)S(1)}, u32[]{:S(2)}, u32[]{:S(2)}) collective-permute-start(f32[4,256]{1,0:T(4,128)S(1)} %fusion.10), channel_id=1, source_target_pairs={{0,2},{1,3},{2,0},{3,1},{4,6},{5,7},{6,4},{7,5},{8,10},{9,11},{10,... | collective-permute-start | bytes 12296 | tf_op jit(solution)/shard_map/ppermute | solution.py:431
  126.4 2.5 %collective-permute-start.8 = (f32[4,256]{1,0:T(4,128)S(1)}, f32[4,256]{1,0:T(4,128)S(1)}, u32[]{:S(2)}, u32[]{:S(2)}) collective-permute-start(f32[4,256]{1,0:T(4,128)S(1)} %fusion.10), channel_id=1, source_target_pairs={{0,3},{1,0},{2,1},{3,2},{4,7},{5,4},{6,5},{7,6},{8,11},{9,8},{10,9... | collective-permute-start | bytes 12296 | tf_op jit(solution)/shard_map/ppermute | solution.py:431
  173.7 1.6 copy-start
Sparse Core Ops, SparseCore 0:
  51.4 32.8 reduce-scatter.1
  122.8 36.6 all-gather.1
